TPU v7x, 128 devices: a whole 4x4x4 slice. The times are simulated.
128 devices in a mesh: dp: 64 (over y, z_hi, x, core), mp: 2 (over z_lo).
Axes of the slice: x: 4, y: 4, z: 4 (z_hi: 2, z_lo: 2; z = z_hi * 2 + z_lo), core: 2. Of those that a mesh axis runs over, the one named last changes fastest.
Arguments:
- img_feat: bfloat16 [13312, 1152], P('dp'), may hold values from -16 to 16
- img_head: bfloat16 [1152, 1152], P(None, 'mp'), may hold values from -0.1875 to 0.1875
- txt_feat: bfloat16 [13312, 1152], P('dp'), may hold values from -6 to 6
- txt_head: bfloat16 [1152, 1152], P('mp'), may hold values from -0.1875 to 0.1875
Outputs:
- grad_img: float32 [13312, 1152], P('dp', 'mp')
- grad_img_head: float32 [1152, 1152], P('dp', 'mp')
- grad_txt: float32 [13312, 1152], P('dp', 'mp')
- grad_txt_head: float32 [1152, 1152], P('mp', 'dp')
All inputs are finite; a program needn't handle non-finite values.
Results may differ from a plain program's by a relative error of at most 0.014.
Values may be sent and summed in bfloat16 or wider, within the bound.
A program may use at most 128 MiB of HBM per device.

v0:
```python
import types

import jax
import jax.numpy as jnp
from jax import lax
from jax.experimental import pallas as pl
from jax.experimental.pallas import tpu as pltpu
from jax.sharding import PartitionSpec as P

LOGIT_SCALE = 10.0
LOGIT_BIAS = -2.5
NORM_EPS = 1e-06

NX = 4
NY = 4
NZ = 2
NC = 2
D = 1152
HALF = D // 2
PAIRS = 208
OWN = PAIRS // 2
WIN = 112
STEP = PAIRS - WIN
TC = NZ * WIN
IMGS = NX * PAIRS
YROWS = D // NY
ZROWS = YROWS // NZ
LAST = ZROWS // (NX * NC)
XWIN = 48
XHALF = NY * NZ * XWIN // 2
FIN = 32
BLOCK = IMGS // 2

NN = ((1,), (0,))
NT = ((1,), (1,))
TN = ((0,), (0,))
BF = jnp.bfloat16
F32 = jnp.float32

SCRATCH = {
    "tf": ((PAIRS, D), BF),
    "th": ((HALF, D), BF),
    "imf": ((PAIRS, D), BF),
    "iht": ((HALF, D), BF),
    "nhf": ((PAIRS, HALF), F32),
    "nhb": ((PAIRS, HALF), BF),
    "rs": ((PAIRS, 128), F32),
    "tpart": ((PAIRS, D), F32),
    "tsend": ((WIN, D), BF),
    "trecv": ((WIN, D), BF),
    "u": ((2, 8, D), F32),
    "tproj": ((WIN, D), F32),
    "tsc": ((WIN, 128), F32),
    "imh": ((NX, 2, PAIRS, HALF), BF),
    "isc": ((PAIRS, 128), F32),
    "img": ((IMGS, D), BF),
    "txt": ((NY, NC * TC, D), BF),
    "w": ((NY, IMGS, NC * TC), BF),
    "gi": ((IMGS, D), F32),
    "xsend": ((3, PAIRS, D), BF),
    "xa": ((WIN, D), BF),
    "xb": ((STEP, D), BF),
    "xr": ((2, PAIRS, D), BF),
    "gtcsend": ((NY, TC, D), BF),
    "gtcrecv": ((NY, TC, D), BF),
    "gt": ((NY, TC, D), F32),
    "gtall": ((NC * TC, D), F32),
    "ysend": ((3, TC, D), BF),
    "ya": ((WIN, D), BF),
    "yb": ((WIN, D), BF),
    "yr": ((2, TC, D), BF),
    "zsend": ((WIN, D), BF),
    "zrecv": ((WIN, D), BF),
    "gown": ((WIN, D), F32),
    "tw": ((2, WIN, D), BF),
    "sw": ((2, WIN, 128), F32),
    "tpg": ((PAIRS, D), BF),
    "sec": ((PAIRS, 128), F32),
    "ghalf": ((PAIRS, HALF), F32),
    "izsend": ((PAIRS, HALF), BF),
    "izrecv": ((PAIRS, HALF), BF),
    "dots": ((2, PAIRS, 128), F32),
    "pg": ((PAIRS, HALF), BF),
    "gip": ((PAIRS, D), F32),
    "gsend": ((PAIRS, HALF), BF),
    "grecv": ((PAIRS, HALF), BF),
    "imft": ((PAIRS, D), BF),
    "nhbt": ((PAIRS, HALF), BF),
    "pgt": ((PAIRS, HALF), BF),
    "tpgt": ((PAIRS, D), BF),
    "h": ((D, HALF), F32),
    "h1send": ((3, 2, XHALF, HALF), BF),
    "h1ab": ((2, XHALF, HALF), BF),
    "h1r": ((2, 2, XHALF, HALF), BF),
    "h1": ((2 * XHALF, HALF), F32),
    "h2send": ((3, 2, XWIN, HALF), BF),
    "h2ab": ((2, XWIN, HALF), BF),
    "h2r": ((2, 2, XWIN, HALF), BF),
    "h2": ((2 * XWIN, HALF), F32),
    "h3send": ((XWIN, HALF), BF),
    "h3recv": ((XWIN, HALF), BF),
    "h4": ((XWIN, HALF), F32),
    "finr": ((FIN, HALF), F32),
}

GROUPS = (
    ("t", 1), ("u", 1), ("img", NX * 2), ("txt", NY * NZ), ("txtc", NY), ("xa", 1), ("xb", 1), ("xr", 2),
    ("iz", 1), ("dots", 1), ("gtc", NY), ("ya", 1), ("yb", 1), ("yr", 2), ("z", 1), ("tw", 1), ("sw", 1),
    ("g", 1), ("imft", 1), ("nhbt", 1), ("pgt", 1), ("tpgt", 1),
    ("h1ab", 2), ("h1r", 2), ("h2ab", 2), ("h2r", 2), ("h3", 1), ("fin", 1),
)
RECVS = {}
total_recvs = 0
for group, many in GROUPS:
    RECVS[group] = total_recvs
    total_recvs += many
total_sends = 80


def dot(a, b, dims):
    return lax.dot_general(a, b, (dims, ((), ())), preferred_element_type=F32)


def rows(i, first=0):
    return pl.ds(pl.multiple_of(first + i * 16, 16), 16)


def rowsum(v):
    return jnp.sum(v, -1, keepdims=True)


def wide(v):
    return jnp.broadcast_to(v, (v.shape[0], 128))


def each(count, body):
    lax.fori_loop(0, count, lambda i, c: (body(i), c)[1], 0)


def kernel(img_feat, img_head_t, txt_feat, txt_head, g_img, g_ih, g_txt, g_th, *scratch):
    s = types.SimpleNamespace(**dict(zip(SCRATCH, scratch)))
    ssem, rsem, lsem = scratch[len(SCRATCH) :]
    dp, m = lax.axis_index("dp"), lax.axis_index("mp")
    core = lax.rem(dp, NC)
    x = lax.rem(dp // NC, NX)
    zh = lax.rem(dp // (NC * NX), NZ)
    y = dp // (NC * NX * NZ)
    om, oc, oz = 1 - m, 1 - core, 1 - zh

    loads = [
        pltpu.make_async_copy(src, dst, lsem.at[at])
        for at, (src, dst) in enumerate(
            ((txt_feat, s.tf), (txt_head, s.th), (img_feat, s.imf), (img_head_t, s.iht))
        )
    ]
    for load in loads:
        load.start()

    def dev(yy=None, zz=None, xx=None, cc=None, mm=None):
        yy = y if yy is None else yy
        zz = zh if zz is None else zz
        xx = x if xx is None else xx
        cc = core if cc is None else cc
        mm = m if mm is None else mm
        return (((yy * NZ + zz) * NX + xx) * NC + cc, mm)

    def other(base, by, size):
        return lax.rem(base + by, size)

    x1, x2, x3 = (other(x, d, NX) for d in (1, 2, 3))
    y1, y2, y3 = (other(y, d, NY) for d in (1, 2, 3))
    mate, twin, far = dev(mm=om), dev(cc=oc), dev(zz=oz, mm=om)
    xup, xdown, yup, ydown = dev(xx=x1), dev(xx=x3), dev(yy=y1), dev(yy=y3)

    used = [0]
    sent = []

    def copy(src, dst, group, at, to):
        used[0] += 1
        return pltpu.make_async_remote_copy(
            src_ref=src,
            dst_ref=dst,
            send_sem=ssem.at[used[0] - 1],
            recv_sem=rsem.at[RECVS[group] + at],
            device_id=to,
            device_id_type=pl.DeviceIdType.MESH,
        )

    def send(c):
        c.start()
        sent.append(c)
        return c

    def arrived(ref, group, at=0):
        pltpu.make_async_remote_copy(
            src_ref=ref,
            dst_ref=ref,
            send_sem=ssem.at[0],
            recv_sem=rsem.at[RECVS[group] + at],
            device_id=twin,
            device_id_type=pl.DeviceIdType.MESH,
        ).wait_recv()

    def pick(whole, which):
        return jnp.where(which == 0, whole[:, :HALF], whole[:, HALF:])

    barrier = pltpu.get_barrier_semaphore()
    friends = [mate, twin, far, dev(zz=oz), xup, xdown, yup, ydown]
    for friend in friends:
        pl.semaphore_signal(barrier, inc=1, device_id=friend, device_id_type=pl.DeviceIdType.MESH)

    loads[0].wait()

    def norm(i):
        r = rows(i)
        t = s.tf[r, :].astype(F32)
        c = t - rowsum(t) * (1.0 / D)
        rs = lax.rsqrt(rowsum(c * c) * (1.0 / D) + NORM_EPS)
        half = pick(c * rs, m)
        s.nhf[r, :] = half
        s.nhb[r, :] = half.astype(BF)
        s.rs[r, :] = wide(rs)

    each(PAIRS // 16, norm)
    loads[1].wait()
    s.tpart[...] = dot(s.nhb[...], s.th[...], NN)

    def tosend(i):
        s.tsend[rows(i), :] = s.tpart[rows(i, om * STEP), :].astype(BF)

    each(WIN // 16, tosend)
    pl.semaphore_wait(barrier, len(friends))
    send(copy(s.tsend, s.trecv, "t", 0, mate))

    loads[2].wait()
    loads[3].wait()
    s.imh[x, m] = dot(s.imf[...], s.iht[...], NT).astype(BF)

    def send_image(xx, half, to):
        send(copy(s.imh.at[xx, half], s.imh.at[xx, half], "img", xx * 2 + half, to))

    def image_arrived(xx, half):
        arrived(s.imh.at[xx, half], "img", xx * 2 + half)

    for to in (mate, xup, xdown):
        send_image(x, m, to)
    s.u[m] = dot(jnp.ones((8, HALF), BF), s.th[...], NN)
    send(copy(s.u.at[m], s.u.at[m], "u", 0, mate))

    nhb_copy = copy(s.nhb, s.nhbt, "nhbt", 0, twin)
    imf_copy = copy(s.imf, s.imft, "imft", 0, twin)
    pg_copy = copy(s.pg, s.pgt, "pgt", 0, twin)
    tpg_copy = copy(s.tpg, s.tpgt, "tpgt", 0, twin)

    @pl.when(core == 0)
    def _():
        nhb_copy.start()

    @pl.when(core == 1)
    def _():
        imf_copy.start()

    arrived(s.trecv, "t")

    def embed_text(i):
        p = s.tpart[rows(i, m * STEP), :] + s.trecv[rows(i), :].astype(F32)
        sc = lax.rsqrt(rowsum(p * p) + NORM_EPS)
        row = m * STEP + i * 16 + lax.broadcasted_iota(jnp.int32, (16, 1), 0)
        mine = (row >= m * OWN) & (row < m * OWN + OWN)
        s.tproj[rows(i), :] = p
        s.tsc[rows(i), :] = wide(sc)
        s.txt[y, rows(i, core * TC + zh * WIN), :] = jnp.where(mine, p * sc, 0.0).astype(BF)

    each(WIN // 16, embed_text)

    def part(yy, zz):
        return s.txt.at[yy, pl.ds(pl.multiple_of(core * TC + zz * WIN, 16), WIN)]

    def side(yy, cc):
        return s.txt.at[yy, pl.ds(pl.multiple_of(cc * TC, 16), TC)]

    def send_text(yy, zz, to):
        send(copy(part(yy, zz), part(yy, zz), "txt", yy * NZ + zz, to))

    def text_arrived(yy, zz):
        arrived(part(yy, zz), "txt", yy * NZ + zz)

    def send_twin(yy):
        send(copy(side(yy, core), side(yy, core), "txtc", yy, twin))

    def twin_arrived(yy):
        arrived(side(yy, oc), "txtc", yy)

    for to in (far, yup, ydown):
        send_text(y, zh, to)

    image_arrived(x, om)
    send_image(x, om, xup)
    send_image(x, om, xdown)

    def embed_images(xx, at, own=False):
        def embed(i):
            r = rows(i)
            p = jnp.concatenate([s.imh[xx, 0, r, :].astype(F32), s.imh[xx, 1, r, :].astype(F32)], axis=1)
            sc = lax.rsqrt(rowsum(p * p) + NORM_EPS)
            if own:
                s.isc[r, :] = wide(sc)
            s.img[rows(i, at * PAIRS), :] = (p * sc).astype(BF)

        each(PAIRS // 16, embed)

    embed_images(x, 0, own=True)

    def zero(i):
        s.gi[rows(i), :] = jnp.zeros((16, D), F32)

    each(IMGS // 16, zero)
    text_arrived(y, oz)
    send_text(y, oz, yup)
    send_text(y, oz, ydown)
    send_twin(y)

    def unit(yy, half, own=False):
        r = pl.ds(pl.multiple_of(half * BLOCK, 16), BLOCK)
        texts = s.txt[yy]
        scores = dot(s.img[r, :], texts, NT)
        weights = 0.5 + 0.5 * jnp.tanh((0.5 * LOGIT_SCALE) * scores + 0.5 * LOGIT_BIAS)
        if own:
            row = lax.broadcasted_iota(jnp.int32, (BLOCK, NC * TC), 0)
            col = lax.broadcasted_iota(jnp.int32, (BLOCK, NC * TC), 1)
            first = core * TC + zh * WIN
            match = (row - col == m * STEP - first) & (col >= first) & (col < first + WIN)
            weights = weights - match.astype(F32)
        weights = weights.astype(BF)
        s.w[yy, r, :] = weights
        s.gi[r, :] += dot(weights, texts, NN)

    image_arrived(x1, 0)
    send_image(x1, 0, xdown)
    image_arrived(x3, 1)
    send_image(x3, 1, xup)
    image_arrived(x1, 1)
    embed_images(x1, 1)
    twin_arrived(y)
    unit(y, 0, own=True)
    image_arrived(x3, 0)
    embed_images(x3, 2)
    text_arrived(y1, 0)
    send_text(y1, 0, ydown)
    text_arrived(y3, 1)
    send_text(y3, 1, yup)
    text_arrived(y1, 1)
    send_twin(y1)
    text_arrived(y3, 0)
    send_twin(y3)
    image_arrived(x2, 0)
    image_arrived(x2, 1)
    embed_images(x2, 3)
    unit(y, 1)
    twin_arrived(y1)
    twin_arrived(y3)
    each(4, lambda i: unit(other(y, 1 + i // 2 * 2, NY), lax.rem(i, 2)))

    text_arrived(y2, 0)
    text_arrived(y2, 1)
    send_twin(y2)
    twin_arrived(y2)
    unit(y2, 1)

    def cast(at, place, add=None, first=0, count=PAIRS):
        def body(i):
            v = s.gi[rows(i, place * PAIRS + first), :]
            if add is not None:
                v = v + add[rows(i), :].astype(F32)
            s.xsend[at, rows(i, first), :] = v.astype(BF)

        each(count // 16, body)

    cast(0, 3)
    send(copy(s.xsend.at[0, pl.ds(0, WIN)], s.xa, "xa", 0, xup))
    send(copy(s.xsend.at[0, pl.ds(WIN, STEP)], s.xb, "xb", 0, xdown))
    unit(y2, 0)

    def text_grad(yy):
        s.gtall[...] = dot(s.w[yy], s.img[...], TN)

        def out(i):
            s.gtcsend[yy, rows(i), :] = s.gtall[rows(i, oc * TC), :].astype(BF)
            s.gt[yy, rows(i), :] = s.gtall[rows(i, core * TC), :]

        each(TC // 16, out)

    def send_back_twin(yy):
        send(copy(s.gtcsend.at[yy], s.gtcrecv.at[yy], "gtc", yy, twin))

    def back_twin_arrived(yy):
        arrived(s.gtcrecv.at[yy], "gtc", yy)

    text_grad(y2)
    send_back_twin(y2)
    text_grad(y1)
    send_back_twin(y1)
    back_twin_arrived(y2)

    def cast_y(at, yy, add=None, zz=0):
        def body(i):
            r = rows(i, zz * WIN)
            v = s.gt[yy, r, :] + s.gtcrecv[yy, r, :].astype(F32)
            if add is not None:
                v = v + add[rows(i), :].astype(F32)
            s.ysend[at, r, :] = v.astype(BF)

        each(WIN // 16, body)

    cast_y(0, y2, zz=0)
    send(copy(s.ysend.at[0, pl.ds(0, WIN)], s.ya, "ya", 0, yup))
    cast_y(0, y2, zz=1)
    send(copy(s.ysend.at[0, pl.ds(WIN, WIN)], s.yb, "yb", 0, ydown))
    cast(1, 1, first=WIN, count=STEP)
    cast(2, 2, first=0, count=WIN)
    arrived(s.xa, "xa")
    cast(1, 1, add=s.xa, first=0, count=WIN)
    send(copy(s.xsend.at[1], s.xr.at[0], "xr", 0, xup))
    arrived(s.xb, "xb")
    cast(2, 2, add=s.xb, first=WIN, count=STEP)
    send(copy(s.xsend.at[2], s.xr.at[1], "xr", 1, xdown))

    def rest(k):
        text_grad(other(y, 3 + k, NY))

    each(2, rest)
    send_back_twin(y3)
    send_back_twin(y)
    back_twin_arrived(y1)
    cast_y(1, y1, zz=1)
    arrived(s.ya, "ya")
    cast_y(1, y1, add=s.ya, zz=0)
    send(copy(s.ysend.at[1], s.yr.at[0], "yr", 0, yup))
    back_twin_arrived(y3)
    cast_y(2, y3, zz=0)
    arrived(s.yb, "yb")
    cast_y(2, y3, add=s.yb, zz=1)
    send(copy(s.ysend.at[2], s.yr.at[1], "yr", 1, ydown))
    back_twin_arrived(y)

    arrived(s.xr.at[0], "xr", 0)
    arrived(s.xr.at[1], "xr", 1)

    def projection(r):
        return jnp.concatenate([s.imh[x, 0, r, :].astype(F32), s.imh[x, 1, r, :].astype(F32)], axis=1)

    def image_sum(i):
        r = rows(i)
        g = s.gi[rows(i), :] + s.xr[0, r, :].astype(F32) + s.xr[1, r, :].astype(F32)
        g = LOGIT_SCALE * g
        s.dots[m, r, :] = wide(rowsum(g * projection(r)))
        s.ghalf[r, :] = pick(g, m)
        s.izsend[r, :] = pick(g, om).astype(BF)

    each(PAIRS // 16, image_sum)
    send(copy(s.dots.at[m], s.dots.at[m], "dots", 0, mate))
    send(copy(s.izsend, s.izrecv, "iz", 0, mate))

    arrived(s.yr.at[0], "yr", 0)
    arrived(s.yr.at[1], "yr", 1)

    def text_sum(r):
        g = s.gt[y, r, :] + s.gtcrecv[y, r, :].astype(F32)
        return g + s.yr[0, r, :].astype(F32) + s.yr[1, r, :].astype(F32)

    def text_far(i):
        s.zsend[rows(i), :] = text_sum(rows(i, oz * WIN)).astype(BF)

    each(WIN // 16, text_far)
    send(copy(s.zsend, s.zrecv, "z", 0, far))

    def text_near(i):
        s.gown[rows(i), :] = text_sum(rows(i, zh * WIN))

    each(WIN // 16, text_near)

    arrived(s.dots.at[om], "dots")
    arrived(s.izrecv, "iz")

    def image_grad(i):
        r = rows(i)
        g = s.ghalf[r, :] + s.izrecv[r, :].astype(F32)
        sc = s.isc[r, :][:, :1]
        total = (s.dots[0, r, :] + s.dots[1, r, :])[:, :1]
        p = s.imh[x, m, r, :].astype(F32)
        s.pg[r, :] = (sc * g - (sc * sc * sc) * p * total).astype(BF)

    each(PAIRS // 16, image_grad)

    @pl.when(core == 1)
    def _():
        pg_copy.start()

    s.gip[...] = dot(s.pg[...], s.iht[...], NN)

    def image_out(i):
        s.gsend[rows(i), :] = pick(s.gip[rows(i), :], om).astype(BF)

    each(PAIRS // 16, image_out)

    arrived(s.zrecv, "z")

    def text_own(i):
        r = rows(i)
        g = LOGIT_SCALE * (s.gown[r, :] + s.zrecv[r, :].astype(F32))
        p = s.tproj[r, :]
        sc = s.tsc[r, :][:, :1]
        v = sc * g - (sc * sc * sc) * p * rowsum(p * g)
        row = m * STEP + i * 16 + lax.broadcasted_iota(jnp.int32, (16, 1), 0)
        mine = (row >= m * OWN) & (row < m * OWN + OWN)
        v = jnp.where(mine, v, 0.0).astype(BF)
        s.tw[m, r, :] = v
        s.sw[m, r, :] = wide(rowsum(v.astype(F32) * p))

    each(WIN // 16, text_own)
    send(copy(s.tw.at[m], s.tw.at[m], "tw", 0, mate))
    send(copy(s.sw.at[m], s.sw.at[m], "sw", 0, mate))
    send(copy(s.gsend, s.grecv, "g", 0, mate))

    class Ring:
        def __init__(self, load, count, bufs, groups, up, down, chunks):
            self.load, self.count, self.chunks = load, count, chunks
            self.out, self.ab, self.back = bufs
            self.groups = groups
            self.used = pl.ds(0, count * 16)
            n = self.used
            self.copies = [
                copy(self.out.at[0, 0, n], self.ab.at[0, n], groups[0], 0, up),
                copy(self.out.at[0, 1, n], self.ab.at[1, n], groups[0], 1, down),
                copy(self.out.at[1, :, n], self.back.at[0, :, n], groups[1], 0, up),
                copy(self.out.at[2, :, n], self.back.at[1, :, n], groups[1], 1, down),
            ]

        def cast(self, at, chunk, half, add=None):
            def body(i):
                v = self.load(chunk, half, i)
                if add is not None:
                    v = v + self.ab[add, rows(i), :].astype(F32)
                self.out[at, half, rows(i), :] = v.astype(BF)

            each(self.count, body)

        def begin(self):
            for half in (0, 1):
                self.cast(0, self.chunks[2], half)
                self.copies[half].start()

        def finish(self, store):
            self.cast(1, self.chunks[1], 1)
            self.cast(2, self.chunks[3], 0)
            arrived(self.ab.at[0, self.used], self.groups[0], 0)
            self.cast(1, self.chunks[1], 0, add=0)
            self.copies[2].start()
            arrived(self.ab.at[1, self.used], self.groups[0], 1)
            self.cast(2, self.chunks[3], 1, add=1)
            self.copies[3].start()
            arrived(self.back.at[0, :, self.used], self.groups[1], 0)
            arrived(self.back.at[1, :, self.used], self.groups[1], 1)
            for half in (0, 1):

                def total(i, half=half):
                    v = self.load(self.chunks[0], half, i) + self.back[0, half, rows(i), :].astype(F32)
                    store(half, i, v + self.back[1, half, rows(i), :].astype(F32))

                each(self.count, total)
            for c in self.copies:
                c.wait_send()

    def store_first(count):
        def store(half, i, v):
            s.h1[rows(i, half * count * 16), :] = v

        return store

    def store_second(half, i, v):
        s.h2[rows(i, half * XWIN), :] = v

    bufs1, bufs2 = (s.h1send, s.h1ab, s.h1r), (s.h2send, s.h2ab, s.h2r)
    xs, ys = (x, x1, x2, x3), (y, y1, y2, y3)
    tall = ZROWS // 16
    image_first = Ring(
        lambda c, half, i: s.h[rows(i, c * YROWS + half * ZROWS), :],
        tall, bufs1, ("h1ab", "h1r"), yup, ydown, ys,
    )
    image_second = Ring(
        lambda c, half, i: s.h1[rows(i, half * ZROWS + c * 32), :],
        XWIN // 16, bufs2, ("h2ab", "h2r"), xup, xdown, xs,
    )
    text_first = Ring(
        lambda c, half, i: s.h[rows(lax.rem(i, 3), (half * NY + i // 3) * ZROWS + c * 32), :],
        XHALF // 16, bufs1, ("h1ab", "h1r"), xup, xdown, xs,
    )
    text_second = Ring(
        lambda c, half, i: s.h1[rows(i, (c * NZ + half) * XWIN), :],
        XWIN // 16, bufs2, ("h2ab", "h2r"), yup, ydown, ys,
    )

    @pl.when(core == 0)
    def _():
        arrived(s.imft, "imft")
        arrived(s.pgt, "pgt")
        s.h[...] = dot(s.imf[...], s.pg[...], TN) + dot(s.imft[...], s.pgt[...], TN)
        image_first.begin()

    arrived(s.tw.at[om], "tw")
    arrived(s.sw.at[om], "sw")
    arrived(s.u.at[om], "u")

    def merge(i):
        lo, hi = jnp.minimum(i, 6), jnp.maximum(i - 6, 0)
        v = jnp.where(i <= 6, s.tw[0, rows(lo), :].astype(F32), 0.0)
        v = v + jnp.where(i >= 6, s.tw[1, rows(hi), :].astype(F32), 0.0)
        s.tpg[rows(i), :] = v.astype(BF)
        v = jnp.where(i <= 6, s.sw[0, rows(lo), :], 0.0)
        s.sec[rows(i), :] = v + jnp.where(i >= 6, s.sw[1, rows(hi), :], 0.0)

    each(PAIRS // 16, merge)

    @pl.when(core == 0)
    def _():
        tpg_copy.start()

    @pl.when(core == 1)
    def _():
        arrived(s.nhbt, "nhbt")
        arrived(s.tpgt, "tpgt")
        s.h[...] = dot(s.tpg[...], s.nhb[...], TN) + dot(s.tpgt[...], s.nhbt[...], TN)
        text_first.begin()

    g_txt[...] = dot(s.tpg[...], s.th[...], NT)

    def text_input(i):
        r = rows(i)
        u = (s.u[0] + s.u[1])[:1, :]
        first = rowsum(s.tpg[r, :].astype(F32) * u) * (1.0 / D)
        second = s.sec[r, :][:, :1] * (1.0 / D)
        g_txt[r, :] = s.rs[r, :][:, :1] * (g_txt[r, :] - first - s.nhf[r, :] * second)

    each(PAIRS // 16, text_input)

    arrived(s.grecv, "g")

    def image_input(i):
        r = rows(i)
        g_img[r, :] = pick(s.gip[r, :], m) + s.grecv[r, :].astype(F32)

    each(PAIRS // 16, image_input)

    @pl.when(core == 0)
    def _():
        image_first.finish(store_first(tall))
        image_second.begin()
        image_second.finish(store_second)
        nhb_copy.wait_send()
        tpg_copy.wait_send()

    @pl.when(core == 1)
    def _():
        text_first.finish(store_first(XHALF // 16))
        text_second.begin()
        text_second.finish(store_second)
        imf_copy.wait_send()
        pg_copy.wait_send()

    def head_far(i):
        s.h3send[rows(i), :] = s.h2[rows(i, oz * XWIN), :].astype(BF)

    each(XWIN // 16, head_far)
    send(copy(s.h3send, s.h3recv, "h3", 0, dev(zz=oz)))
    arrived(s.h3recv, "h3")

    def head_near(i):
        s.h4[rows(i), :] = s.h2[rows(i, zh * XWIN), :] + s.h3recv[rows(i), :].astype(F32)

    each(XWIN // 16, head_near)
    theirs = s.h4.at[pl.ds(pl.multiple_of(oc * 16, 16), FIN)]
    send(copy(theirs, s.finr, "fin", 0, twin))
    own = pltpu.roll(s.h4[...], lax.rem(XWIN - 4 * x - LAST * core, XWIN), 0)[:LAST, :]
    arrived(s.finr, "fin")
    got = pltpu.roll(s.finr[...], lax.rem(FIN - 4 * x - 2 * core, FIN), 0)[:LAST, :]
    g_ih[...] = jnp.where(core == 0, own, got)
    g_th[...] = jnp.where(core == 0, got, own)

    for c in sent:
        c.wait_send()


def per_device(img_feat, img_head, txt_feat, txt_head):
    vmem = pl.BlockSpec(memory_space=pltpu.VMEM)
    g_img, g_ih, g_txt, g_th = pl.pallas_call(
        kernel,
        out_shape=(
            jax.ShapeDtypeStruct((PAIRS, HALF), F32),
            jax.ShapeDtypeStruct((LAST, HALF), F32),
            jax.ShapeDtypeStruct((PAIRS, HALF), F32),
            jax.ShapeDtypeStruct((LAST, HALF), F32),
        ),
        in_specs=[pl.BlockSpec(memory_space=pl.ANY)] * 4,
        out_specs=(vmem,) * 4,
        scratch_shapes=[pltpu.VMEM(shape, kind) for shape, kind in SCRATCH.values()]
        + [pltpu.SemaphoreType.DMA((total_sends,)), pltpu.SemaphoreType.DMA((total_recvs,))]
        + [pltpu.SemaphoreType.DMA((4,))],
        compiler_params=pltpu.CompilerParams(
            collective_id=0, has_side_effects=True, vmem_limit_bytes=60 * 1024 * 1024
        ),
        cost_estimate=pl.CostEstimate(flops=14 * 10**9, bytes_accessed=5 * 10**6, transcendentals=0),
    )(img_feat, img_head.T, txt_feat, txt_head)
    return g_img, g_ih, g_txt, g_th.T


def solution(mesh):
    in_specs = (P("dp", None), P(None, "mp"), P("dp", None), P("mp", None))
    out_specs = (P("dp", "mp"), P("dp", "mp"), P("dp", "mp"), P("mp", "dp"))
    return jax.shard_map(
        per_device, mesh=mesh, in_specs=in_specs, out_specs=out_specs, check_vma=False
    )
```

profile of v0, /device:TPU:1, one launch (start us, length us, event | category | flops | bytes accessed | tf_op | source)
XLA Modules:
  0.0 130.3 jit_solution(6829002273721766204)
XLA Ops:
  0.6 124.8 %shard_map.75 = (f32[208,576]{1,0:T(8,128)}, f32[18,576]{1,0:T(8,128)}, f32[208,576]{1,0:T(8,128)}, f32[18,576]{1,0:T(8,128)}) custom-call(bf16[208,1152]{1,0:T(8,128)(2,1)} %img_feat.1, bf16[576,1152]{1,0:T(8,128)(2,1)} %bitcast.3, bf16[208,1152]{1,0:T(8,128)(2,1)} %txt_feat.1, bf16[576,1152]{1,0:T(8,128)(2,1)} %txt_head.1), custom_call_target="tpu_custom_call" | custom-call | flops 14000000000 | bytes 5000000 | tf_op jit(solution)/shard_map/pallas_call | solution.py:695
  125.4 0.0 copy-start
  125.4 0.0 copy-start.1
  125.5 1.9 %copy.12 = f32[208,576]{1,0:T(8,128)} copy(f32[208,576]{1,0:T(8,128)} %get-tuple-element.16) | data formatting | bytes 958464
  127.4 1.5 %copy.13 = f32[18,576]{1,0:T(8,128)} copy(f32[18,576]{1,0:T(8,128)} %get-tuple-element.17) | data formatting | bytes 82944
  128.8 0.0 copy-done
  128.8 0.8 copy.14
  129.6 0.0 copy-done.1
  129.6 0.6 copy.15
Async XLA Ops:
  125.4 3.4 %copy-start = (f32[208,576]{1,0:T(8,128)S(1)}, f32[208,576]{1,0:T(8,128)}, u32[]{:S(2)}) copy-start(f32[208,576]{1,0:T(8,128)} %get-tuple-element.18) | copy-start | bytes 1437700
  125.4 4.2 %copy-start.1 = (f32[18,576]{1,0:T(8,128)S(1)}, f32[18,576]{1,0:T(8,128)}, u32[]{:S(2)}) copy-start(f32[18,576]{1,0:T(8,128)} %get-tuple-element.11) | copy-start | bytes 124420
where the time goes:
time: 130 us
  Pallas kernels  125 us (96%)
  local copies, waits for them, and re-layouts  4.81 us (4%)
    pallas_call x1, Pallas kernels, per_device(): pl.pallas_call(kernel, out_shape=(jax.ShapeDtypeStruct((PAIRS, HALF), F32...  125 us
    unnamed x8, local copies, waits for them, and re-layouts  4.81 us

commit v1 on v0

--- a/solution.py
+++ b/solution.py
@@ -30,6 +30,9 @@
 XHALF = NY * NZ * XWIN // 2
 FIN = 32
 BLOCK = IMGS // 2
+CUT = 64
+IMAGE_PARTS = ((0, WIN), (WIN, STEP))
+TEXT_PARTS = ((0, CUT), (CUT, WIN - CUT))
 
 NN = ((1,), (0,))
 NT = ((1,), (1,))
@@ -66,8 +69,8 @@
     "gt": ((NY, TC, D), F32),
     "gtall": ((NC * TC, D), F32),
     "ysend": ((3, TC, D), BF),
-    "ya": ((WIN, D), BF),
-    "yb": ((WIN, D), BF),
+    "ya": ((NZ, CUT, D), BF),
+    "yb": ((NZ, WIN - CUT, D), BF),
     "yr": ((2, TC, D), BF),
     "zsend": ((WIN, D), BF),
     "zrecv": ((WIN, D), BF),
@@ -75,7 +78,6 @@
     "tw": ((2, WIN, D), BF),
     "sw": ((2, WIN, 128), F32),
     "tpg": ((PAIRS, D), BF),
-    "sec": ((PAIRS, 128), F32),
     "ghalf": ((PAIRS, HALF), F32),
     "izsend": ((PAIRS, HALF), BF),
     "izrecv": ((PAIRS, HALF), BF),
@@ -104,17 +106,17 @@
 }
 
 GROUPS = (
-    ("t", 1), ("u", 1), ("img", NX * 2), ("txt", NY * NZ), ("txtc", NY), ("xa", 1), ("xb", 1), ("xr", 2),
-    ("iz", 1), ("dots", 1), ("gtc", NY), ("ya", 1), ("yb", 1), ("yr", 2), ("z", 1), ("tw", 1), ("sw", 1),
+    ("t", 1), ("u", 1), ("img", NX * 4), ("txt", NY * NZ * 2), ("txtc", NY), ("xa", 1), ("xb", 1), ("xr", 4),
+    ("iz", 1), ("dots", 1), ("gtc", NY), ("ya", 2), ("yb", 2), ("yr", 8), ("z", 2), ("tw", 2), ("sw", 1),
     ("g", 1), ("imft", 1), ("nhbt", 1), ("pgt", 1), ("tpgt", 1),
-    ("h1ab", 2), ("h1r", 2), ("h2ab", 2), ("h2r", 2), ("h3", 1), ("fin", 1),
+    ("h1ab", 2), ("h1r", 4), ("h2ab", 2), ("h2r", 4), ("h3", 1), ("fin", 1),
 )
 RECVS = {}
 total_recvs = 0
 for group, many in GROUPS:
     RECVS[group] = total_recvs
     total_recvs += many
-total_sends = 80
+total_sends = 128
 
 
 def dot(a, b, dims):
@@ -236,11 +238,23 @@
     loads[3].wait()
     s.imh[x, m] = dot(s.imf[...], s.iht[...], NT).astype(BF)
 
-    def send_image(xx, half, to):
-        send(copy(s.imh.at[xx, half], s.imh.at[xx, half], "img", xx * 2 + half, to))
-
-    def image_arrived(xx, half):
-        arrived(s.imh.at[xx, half], "img", xx * 2 + half)
+    def image_part(xx, half, cut):
+        if cut is None:
+            return s.imh.at[xx, half]
+        return s.imh.at[xx, half, pl.ds(*IMAGE_PARTS[cut])]
+
+    def send_image(xx, half, to, cut=None):
+        ref = image_part(xx, half, cut)
+        send(copy(ref, ref, "img", xx * 4 + half * 2 + (cut or 0), to))
+
+    def image_arrived(xx, half, cut=None):
+        arrived(image_part(xx, half, cut), "img", xx * 4 + half * 2 + (cut or 0))
+
+    def forward_image(half):
+        image_arrived(x1, half)
+        send_image(x1, half, xdown, 0)
+        image_arrived(x3, half)
+        send_image(x3, half, xup, 1)
 
     for to in (mate, xup, xdown):
         send_image(x, m, to)
@@ -273,17 +287,25 @@
 
     each(WIN // 16, embed_text)
 
-    def part(yy, zz):
-        return s.txt.at[yy, pl.ds(pl.multiple_of(core * TC + zz * WIN, 16), WIN)]
+    def part(yy, zz, cut=None):
+        first, count = (0, WIN) if cut is None else TEXT_PARTS[cut]
+        return s.txt.at[yy, pl.ds(pl.multiple_of(core * TC + zz * WIN + first, 16), count)]
 
     def side(yy, cc):
         return s.txt.at[yy, pl.ds(pl.multiple_of(cc * TC, 16), TC)]
 
-    def send_text(yy, zz, to):
-        send(copy(part(yy, zz), part(yy, zz), "txt", yy * NZ + zz, to))
-
-    def text_arrived(yy, zz):
-        arrived(part(yy, zz), "txt", yy * NZ + zz)
+    def send_text(yy, zz, to, cut=None):
+        ref = part(yy, zz, cut)
+        send(copy(ref, ref, "txt", yy * 4 + zz * 2 + (cut or 0), to))
+
+    def text_arrived(yy, zz, cut=None):
+        arrived(part(yy, zz, cut), "txt", yy * 4 + zz * 2 + (cut or 0))
+
+    def forward_text(zz):
+        text_arrived(y1, zz)
+        send_text(y1, zz, ydown, 0)
+        text_arrived(y3, zz)
+        send_text(y3, zz, yup, 1)
 
     def send_twin(yy):
         send(copy(side(yy, core), side(yy, core), "txtc", yy, twin))
@@ -293,6 +315,12 @@
 
     for to in (far, yup, ydown):
         send_text(y, zh, to)
+
+    def zero(i):
+        s.gi[rows(i), :] = jnp.zeros((16, D), F32)
+
+    each(IMGS // 16, zero)
+    forward_image(m)
 
     image_arrived(x, om)
     send_image(x, om, xup)
@@ -311,14 +339,11 @@
 
     embed_images(x, 0, own=True)
 
-    def zero(i):
-        s.gi[rows(i), :] = jnp.zeros((16, D), F32)
-
-    each(IMGS // 16, zero)
     text_arrived(y, oz)
     send_text(y, oz, yup)
     send_text(y, oz, ydown)
     send_twin(y)
+    forward_text(zh)
 
     def unit(yy, half, own=False):
         r = pl.ds(pl.multiple_of(half * BLOCK, 16), BLOCK)
@@ -335,35 +360,27 @@
         s.w[yy, r, :] = weights
         s.gi[r, :] += dot(weights, texts, NN)
 
-    image_arrived(x1, 0)
-    send_image(x1, 0, xdown)
-    image_arrived(x3, 1)
-    send_image(x3, 1, xup)
-    image_arrived(x1, 1)
+    forward_image(om)
     embed_images(x1, 1)
+    embed_images(x3, 2)
+    forward_text(oz)
+    send_twin(y1)
+    send_twin(y3)
     twin_arrived(y)
     unit(y, 0, own=True)
-    image_arrived(x3, 0)
-    embed_images(x3, 2)
-    text_arrived(y1, 0)
-    send_text(y1, 0, ydown)
-    text_arrived(y3, 1)
-    send_text(y3, 1, yup)
-    text_arrived(y1, 1)
-    send_twin(y1)
-    text_arrived(y3, 0)
-    send_twin(y3)
-    image_arrived(x2, 0)
-    image_arrived(x2, 1)
-    embed_images(x2, 3)
-    unit(y, 1)
     twin_arrived(y1)
     twin_arrived(y3)
-    each(4, lambda i: unit(other(y, 1 + i // 2 * 2, NY), lax.rem(i, 2)))
-
-    text_arrived(y2, 0)
-    text_arrived(y2, 1)
+    each(2, lambda i: unit(other(y, 1 + 2 * i, NY), 0))
+    for zz in range(NZ):
+        for half in (0, 1):
+            text_arrived(y2, zz, half)
     send_twin(y2)
+    for half in (0, 1):
+        for cut in (0, 1):
+            image_arrived(x2, half, cut)
+    embed_images(x2, 3)
+    each(3, lambda i: unit(other(y, i + i // 2, NY), 1))
+
     twin_arrived(y2)
     unit(y2, 1)
 
@@ -376,10 +393,21 @@
 
         each(count // 16, body)
 
-    cast(0, 3)
-    send(copy(s.xsend.at[0, pl.ds(0, WIN)], s.xa, "xa", 0, xup))
-    send(copy(s.xsend.at[0, pl.ds(WIN, STEP)], s.xb, "xb", 0, xdown))
+    for half in (0, 1):
+        first, count = IMAGE_PARTS[half]
+        cast(0, 3, first=first, count=count)
+        to, at = ((xup, s.xa), (xdown, s.xb))[half]
+        send(copy(s.xsend.at[0, pl.ds(first, count)], at, ("xa", "xb")[half], 0, to))
+
+    def image_back(at, place, half, to, add=None):
+        first, count = IMAGE_PARTS[half]
+        cast(at, place, add=add, first=first, count=count)
+        r = pl.ds(first, count)
+        send(copy(s.xsend.at[at, r], s.xr.at[at - 1, r], "xr", (at - 1) * 2 + half, to))
+
+    image_back(2, 2, 0, xdown)
     unit(y2, 0)
+    image_back(1, 1, 1, xup)
 
     def text_grad(yy):
         s.gtall[...] = dot(s.w[yy], s.img[...], TN)
@@ -400,51 +428,52 @@
     send_back_twin(y2)
     text_grad(y1)
     send_back_twin(y1)
+    arrived(s.xa, "xa")
+    image_back(1, 1, 0, xup, add=s.xa)
+    arrived(s.xb, "xb")
+    image_back(2, 2, 1, xdown, add=s.xb)
     back_twin_arrived(y2)
 
-    def cast_y(at, yy, add=None, zz=0):
+    def text_back(at, yy, zz, half, dst, group, index, to, add=None):
+        first, count = TEXT_PARTS[half]
+
         def body(i):
-            r = rows(i, zz * WIN)
+            r = rows(i, zz * WIN + first)
             v = s.gt[yy, r, :] + s.gtcrecv[yy, r, :].astype(F32)
             if add is not None:
-                v = v + add[rows(i), :].astype(F32)
+                v = v + add[zz, rows(i), :].astype(F32)
             s.ysend[at, r, :] = v.astype(BF)
 
-        each(WIN // 16, body)
-
-    cast_y(0, y2, zz=0)
-    send(copy(s.ysend.at[0, pl.ds(0, WIN)], s.ya, "ya", 0, yup))
-    cast_y(0, y2, zz=1)
-    send(copy(s.ysend.at[0, pl.ds(WIN, WIN)], s.yb, "yb", 0, ydown))
-    cast(1, 1, first=WIN, count=STEP)
-    cast(2, 2, first=0, count=WIN)
-    arrived(s.xa, "xa")
-    cast(1, 1, add=s.xa, first=0, count=WIN)
-    send(copy(s.xsend.at[1], s.xr.at[0], "xr", 0, xup))
-    arrived(s.xb, "xb")
-    cast(2, 2, add=s.xb, first=WIN, count=STEP)
-    send(copy(s.xsend.at[2], s.xr.at[1], "xr", 1, xdown))
-
-    def rest(k):
-        text_grad(other(y, 3 + k, NY))
-
-    each(2, rest)
+        each(count // 16, body)
+        r = pl.ds(pl.multiple_of(zz * WIN + first, 16), count)
+        send(copy(s.ysend.at[at, r], dst(r), group, index, to))
+
+    def text_back_to(at, yy, zz, half, to, add=None):
+        text_back(at, yy, zz, half, lambda r: s.yr.at[at - 1, r], "yr", (at - 1) * 4 + zz * 2 + half, to, add)
+
+    for zz in (oz, zh):
+        text_back(0, y2, zz, 0, lambda r, zz=zz: s.ya.at[zz], "ya", zz, yup)
+        text_back(0, y2, zz, 1, lambda r, zz=zz: s.yb.at[zz], "yb", zz, ydown)
+    text_grad(y3)
     send_back_twin(y3)
+    back_twin_arrived(y1)
+    for zz in (oz, zh):
+        text_back_to(1, y1, zz, 1, yup)
+    back_twin_arrived(y3)
+    for zz in (oz, zh):
+        text_back_to(2, y3, zz, 0, ydown)
+    text_grad(y)
     send_back_twin(y)
-    back_twin_arrived(y1)
-    cast_y(1, y1, zz=1)
-    arrived(s.ya, "ya")
-    cast_y(1, y1, add=s.ya, zz=0)
-    send(copy(s.ysend.at[1], s.yr.at[0], "yr", 0, yup))
-    back_twin_arrived(y3)
-    cast_y(2, y3, zz=0)
-    arrived(s.yb, "yb")
-    cast_y(2, y3, add=s.yb, zz=1)
-    send(copy(s.ysend.at[2], s.yr.at[1], "yr", 1, ydown))
+    for zz in (oz, zh):
+        arrived(s.ya.at[zz], "ya", zz)
+        text_back_to(1, y1, zz, 0, yup, add=s.ya)
+        arrived(s.yb.at[zz], "yb", zz)
+        text_back_to(2, y3, zz, 1, ydown, add=s.yb)
     back_twin_arrived(y)
 
-    arrived(s.xr.at[0], "xr", 0)
-    arrived(s.xr.at[1], "xr", 1)
+    for way in (0, 1):
+        for half in (0, 1):
+            arrived(s.xr.at[way, pl.ds(*IMAGE_PARTS[half])], "xr", way * 2 + half)
 
     def projection(r):
         return jnp.concatenate([s.imh[x, 0, r, :].astype(F32), s.imh[x, 1, r, :].astype(F32)], axis=1)
@@ -461,8 +490,12 @@
     send(copy(s.dots.at[m], s.dots.at[m], "dots", 0, mate))
     send(copy(s.izsend, s.izrecv, "iz", 0, mate))
 
-    arrived(s.yr.at[0], "yr", 0)
-    arrived(s.yr.at[1], "yr", 1)
+    def back_arrived(zz):
+        for way in (0, 1):
+            for half in (0, 1):
+                first, count = TEXT_PARTS[half]
+                r = pl.ds(pl.multiple_of(zz * WIN + first, 16), count)
+                arrived(s.yr.at[way, r], "yr", way * 4 + zz * 2 + half)
 
     def text_sum(r):
         g = s.gt[y, r, :] + s.gtcrecv[y, r, :].astype(F32)
@@ -471,39 +504,19 @@
     def text_far(i):
         s.zsend[rows(i), :] = text_sum(rows(i, oz * WIN)).astype(BF)
 
-    each(WIN // 16, text_far)
-    send(copy(s.zsend, s.zrecv, "z", 0, far))
+    back_arrived(oz)
+    for half in (0, 1):
+        first, count = TEXT_PARTS[half]
+        each(count // 16, lambda i, first=first: text_far(i + first // 16))
+        r = pl.ds(first, count)
+        send(copy(s.zsend.at[r], s.zrecv.at[r], "z", half, far))
+    back_arrived(zh)
 
     def text_near(i):
         s.gown[rows(i), :] = text_sum(rows(i, zh * WIN))
 
     each(WIN // 16, text_near)
 
-    arrived(s.dots.at[om], "dots")
-    arrived(s.izrecv, "iz")
-
-    def image_grad(i):
-        r = rows(i)
-        g = s.ghalf[r, :] + s.izrecv[r, :].astype(F32)
-        sc = s.isc[r, :][:, :1]
-        total = (s.dots[0, r, :] + s.dots[1, r, :])[:, :1]
-        p = s.imh[x, m, r, :].astype(F32)
-        s.pg[r, :] = (sc * g - (sc * sc * sc) * p * total).astype(BF)
-
-    each(PAIRS // 16, image_grad)
-
-    @pl.when(core == 1)
-    def _():
-        pg_copy.start()
-
-    s.gip[...] = dot(s.pg[...], s.iht[...], NN)
-
-    def image_out(i):
-        s.gsend[rows(i), :] = pick(s.gip[rows(i), :], om).astype(BF)
-
-    each(PAIRS // 16, image_out)
-
-    arrived(s.zrecv, "z")
 
     def text_own(i):
         r = rows(i)
@@ -517,10 +530,30 @@
         s.tw[m, r, :] = v
         s.sw[m, r, :] = wide(rowsum(v.astype(F32) * p))
 
-    each(WIN // 16, text_own)
-    send(copy(s.tw.at[m], s.tw.at[m], "tw", 0, mate))
+    for half in (0, 1):
+        first, count = TEXT_PARTS[half]
+        r = pl.ds(first, count)
+        arrived(s.zrecv.at[r], "z", half)
+        each(count // 16, lambda i, first=first: text_own(i + first // 16))
+        send(copy(s.tw.at[m, r], s.tw.at[m, r], "tw", half, mate))
     send(copy(s.sw.at[m], s.sw.at[m], "sw", 0, mate))
-    send(copy(s.gsend, s.grecv, "g", 0, mate))
+
+    arrived(s.dots.at[om], "dots")
+    arrived(s.izrecv, "iz")
+
+    def image_grad(i):
+        r = rows(i)
+        g = s.ghalf[r, :] + s.izrecv[r, :].astype(F32)
+        sc = s.isc[r, :][:, :1]
+        total = (s.dots[0, r, :] + s.dots[1, r, :])[:, :1]
+        p = s.imh[x, m, r, :].astype(F32)
+        s.pg[r, :] = (sc * g - (sc * sc * sc) * p * total).astype(BF)
+
+    each(PAIRS // 16, image_grad)
+
+    @pl.when(core == 1)
+    def _():
+        pg_copy.start()
 
     class Ring:
         def __init__(self, load, count, bufs, groups, up, down, chunks):
@@ -532,8 +565,10 @@
             self.copies = [
                 copy(self.out.at[0, 0, n], self.ab.at[0, n], groups[0], 0, up),
                 copy(self.out.at[0, 1, n], self.ab.at[1, n], groups[0], 1, down),
-                copy(self.out.at[1, :, n], self.back.at[0, :, n], groups[1], 0, up),
-                copy(self.out.at[2, :, n], self.back.at[1, :, n], groups[1], 1, down),
+                copy(self.out.at[1, 1, n], self.back.at[0, 1, n], groups[1], 1, up),
+                copy(self.out.at[2, 0, n], self.back.at[1, 0, n], groups[1], 2, down),
+                copy(self.out.at[1, 0, n], self.back.at[0, 0, n], groups[1], 0, up),
+                copy(self.out.at[2, 1, n], self.back.at[1, 1, n], groups[1], 3, down),
             ]
 
         def cast(self, at, chunk, half, add=None):
@@ -549,18 +584,23 @@
             for half in (0, 1):
                 self.cast(0, self.chunks[2], half)
                 self.copies[half].start()
-
-        def finish(self, store):
             self.cast(1, self.chunks[1], 1)
+            self.copies[2].start()
             self.cast(2, self.chunks[3], 0)
+            self.copies[3].start()
+
+        def pass_on(self):
             arrived(self.ab.at[0, self.used], self.groups[0], 0)
             self.cast(1, self.chunks[1], 0, add=0)
-            self.copies[2].start()
+            self.copies[4].start()
             arrived(self.ab.at[1, self.used], self.groups[0], 1)
             self.cast(2, self.chunks[3], 1, add=1)
-            self.copies[3].start()
-            arrived(self.back.at[0, :, self.used], self.groups[1], 0)
-            arrived(self.back.at[1, :, self.used], self.groups[1], 1)
+            self.copies[5].start()
+
+        def finish(self, store):
+            for way in (0, 1):
+                for half in (0, 1):
+                    arrived(self.back.at[way, half, self.used], self.groups[1], way * 2 + half)
             for half in (0, 1):
 
                 def total(i, half=half):
@@ -606,18 +646,16 @@
         arrived(s.pgt, "pgt")
         s.h[...] = dot(s.imf[...], s.pg[...], TN) + dot(s.imft[...], s.pgt[...], TN)
         image_first.begin()
-
-    arrived(s.tw.at[om], "tw")
-    arrived(s.sw.at[om], "sw")
-    arrived(s.u.at[om], "u")
+        image_first.pass_on()
+
+    for half in (0, 1):
+        arrived(s.tw.at[om, pl.ds(*TEXT_PARTS[half])], "tw", half)
 
     def merge(i):
         lo, hi = jnp.minimum(i, 6), jnp.maximum(i - 6, 0)
         v = jnp.where(i <= 6, s.tw[0, rows(lo), :].astype(F32), 0.0)
         v = v + jnp.where(i >= 6, s.tw[1, rows(hi), :].astype(F32), 0.0)
         s.tpg[rows(i), :] = v.astype(BF)
-        v = jnp.where(i <= 6, s.sw[0, rows(lo), :], 0.0)
-        s.sec[rows(i), :] = v + jnp.where(i >= 6, s.sw[1, rows(hi), :], 0.0)
 
     each(PAIRS // 16, merge)
 
@@ -632,13 +670,30 @@
         s.h[...] = dot(s.tpg[...], s.nhb[...], TN) + dot(s.tpgt[...], s.nhbt[...], TN)
         text_first.begin()
 
+    s.gip[...] = dot(s.pg[...], s.iht[...], NN)
+
+    def image_out(i):
+        s.gsend[rows(i), :] = pick(s.gip[rows(i), :], om).astype(BF)
+
+    each(PAIRS // 16, image_out)
+
+    send(copy(s.gsend, s.grecv, "g", 0, mate))
+
+    @pl.when(core == 1)
+    def _():
+        text_first.pass_on()
+
+    arrived(s.sw.at[om], "sw")
+    arrived(s.u.at[om], "u")
     g_txt[...] = dot(s.tpg[...], s.th[...], NT)
 
     def text_input(i):
         r = rows(i)
         u = (s.u[0] + s.u[1])[:1, :]
         first = rowsum(s.tpg[r, :].astype(F32) * u) * (1.0 / D)
-        second = s.sec[r, :][:, :1] * (1.0 / D)
+        lo, hi = jnp.minimum(i, 6), jnp.maximum(i - 6, 0)
+        second = jnp.where(i <= 6, s.sw[0, rows(lo), :], 0.0) + jnp.where(i >= 6, s.sw[1, rows(hi), :], 0.0)
+        second = second[:, :1] * (1.0 / D)
         g_txt[r, :] = s.rs[r, :][:, :1] * (g_txt[r, :] - first - s.nhf[r, :] * second)
 
     each(PAIRS // 16, text_input)
@@ -655,6 +710,7 @@
     def _():
         image_first.finish(store_first(tall))
         image_second.begin()
+        image_second.pass_on()
         image_second.finish(store_second)
         nhb_copy.wait_send()
         tpg_copy.wait_send()
@@ -663,6 +719,7 @@
     def _():
         text_first.finish(store_first(XHALF // 16))
         text_second.begin()
+        text_second.pass_on()
         text_second.finish(store_second)
         imf_copy.wait_send()
         pg_copy.wait_send()

time: 130 us -> 121 us (0.931)
  Pallas kernels: 125 us -> 115 us
    pallas_call x1, Pallas kernels: 125 us -> 115 us  [per_device(): pl.pallas_call(kernel, out_shape=(jax.ShapeDtypeStruct((PAIRS, HALF), F32...]
where the time goes in v1:
time: 121 us; the launch traced here: 120 us
  Pallas kernels  115 us (95%)
  local copies, waits for them, and re-layouts  4.81 us (4%)
    pallas_call x1, Pallas kernels, per_device(): pl.pallas_call(kernel, out_shape=(jax.ShapeDtypeStruct((PAIRS, HALF), F32...  115 us
    unnamed x8, local copies, waits for them, and re-layouts  4.81 us

profile of v1, /device:TPU:1, one launch (start us, length us, event | category | flops | bytes accessed | tf_op | source)
XLA Modules:
  0.0 120.5 jit_solution(5741816159030002587)
XLA Ops:
  0.6 115.0 %shard_map.75 = (f32[208,576]{1,0:T(8,128)}, f32[18,576]{1,0:T(8,128)}, f32[208,576]{1,0:T(8,128)}, f32[18,576]{1,0:T(8,128)}) custom-call(bf16[208,1152]{1,0:T(8,128)(2,1)} %img_feat.1, bf16[576,1152]{1,0:T(8,128)(2,1)} %bitcast.3, bf16[208,1152]{1,0:T(8,128)(2,1)} %txt_feat.1, bf16[576,1152]{1,0:T(8,128)(2,1)} %txt_head.1), custom_call_target="tpu_custom_call" | custom-call | flops 14000000000 | bytes 5000000 | tf_op jit(solution)/shard_map/pallas_call | solution.py:752
  115.6 0.0 copy-start
  115.6 0.0 copy-start.1
  115.6 1.9 %copy.12 = f32[208,576]{1,0:T(8,128)} copy(f32[208,576]{1,0:T(8,128)} %get-tuple-element.16) | data formatting | bytes 958464
  117.6 1.5 %copy.13 = f32[18,576]{1,0:T(8,128)} copy(f32[18,576]{1,0:T(8,128)} %get-tuple-element.17) | data formatting | bytes 82944
  119.0 0.0 copy-done
  119.0 0.8 copy.14
  119.8 0.0 copy-done.1
  119.8 0.6 copy.15
Async XLA Ops:
  115.6 3.4 %copy-start = (f32[208,576]{1,0:T(8,128)S(1)}, f32[208,576]{1,0:T(8,128)}, u32[]{:S(2)}) copy-start(f32[208,576]{1,0:T(8,128)} %get-tuple-element.18) | copy-start | bytes 1437700
  115.6 4.2 %copy-start.1 = (f32[18,576]{1,0:T(8,128)S(1)}, f32[18,576]{1,0:T(8,128)}, u32[]{:S(2)}) copy-start(f32[18,576]{1,0:T(8,128)} %get-tuple-element.11) | copy-start | bytes 124420

commit v2 on v1

--- a/solution.py
+++ b/solution.py
@@ -29,10 +29,12 @@
 XWIN = 48
 XHALF = NY * NZ * XWIN // 2
 FIN = 32
-BLOCK = IMGS // 2
 CUT = 64
 IMAGE_PARTS = ((0, WIN), (WIN, STEP))
 TEXT_PARTS = ((0, CUT), (CUT, WIN - CUT))
+Z_PARTS = ((0, 32), (32, 32), (64, 48))
+
+COLUMNS = ((0, 256), (256, HALF - 256))
 
 NN = ((1,), (0,))
 NT = ((1,), (1,))
@@ -92,12 +94,10 @@
     "tpgt": ((PAIRS, D), BF),
     "h": ((D, HALF), F32),
     "h1send": ((3, 2, XHALF, HALF), BF),
-    "h1ab": ((2, XHALF, HALF), BF),
-    "h1r": ((2, 2, XHALF, HALF), BF),
+    "h1r": ((3, 2, XHALF, HALF), BF),
     "h1": ((2 * XHALF, HALF), F32),
     "h2send": ((3, 2, XWIN, HALF), BF),
-    "h2ab": ((2, XWIN, HALF), BF),
-    "h2r": ((2, 2, XWIN, HALF), BF),
+    "h2r": ((3, 2, XWIN, HALF), BF),
     "h2": ((2 * XWIN, HALF), F32),
     "h3send": ((XWIN, HALF), BF),
     "h3recv": ((XWIN, HALF), BF),
@@ -106,17 +106,17 @@
 }
 
 GROUPS = (
-    ("t", 1), ("u", 1), ("img", NX * 4), ("txt", NY * NZ * 2), ("txtc", NY), ("xa", 1), ("xb", 1), ("xr", 4),
-    ("iz", 1), ("dots", 1), ("gtc", NY), ("ya", 2), ("yb", 2), ("yr", 8), ("z", 2), ("tw", 2), ("sw", 1),
+    ("t", 2), ("u", 1), ("img", NX * 4), ("txt", NY * NZ * 2), ("txtc", NY * NZ), ("xa", 1), ("xb", 1), ("xr", 4),
+    ("iz", 1), ("dots", 1), ("gtc", NY), ("ya", 2), ("yb", 2), ("yr", 8), ("z", 3), ("tw", 3), ("sw", 1),
     ("g", 1), ("imft", 1), ("nhbt", 1), ("pgt", 1), ("tpgt", 1),
-    ("h1ab", 2), ("h1r", 4), ("h2ab", 2), ("h2r", 4), ("h3", 1), ("fin", 1),
+    ("h1r", 6), ("h2r", 6), ("h3", 1), ("fin", 1),
 )
 RECVS = {}
 total_recvs = 0
 for group, many in GROUPS:
     RECVS[group] = total_recvs
     total_recvs += many
-total_sends = 128
+total_sends = 160
 
 
 def dot(a, b, dims):
@@ -207,7 +207,7 @@
         return jnp.where(which == 0, whole[:, :HALF], whole[:, HALF:])
 
     barrier = pltpu.get_barrier_semaphore()
-    friends = [mate, twin, far, dev(zz=oz), xup, xdown, yup, ydown]
+    friends = [mate, twin, far, dev(zz=oz), xup, xdown, yup, ydown, dev(xx=x2), dev(yy=y2)]
     for friend in friends:
         pl.semaphore_signal(barrier, inc=1, device_id=friend, device_id_type=pl.DeviceIdType.MESH)
 
@@ -232,7 +232,9 @@
 
     each(WIN // 16, tosend)
     pl.semaphore_wait(barrier, len(friends))
-    send(copy(s.tsend, s.trecv, "t", 0, mate))
+    for half, where in enumerate(TEXT_PARTS):
+        r = pl.ds(*where)
+        send(copy(s.tsend.at[r], s.trecv.at[r], "t", half, mate))
 
     loads[2].wait()
     loads[3].wait()
@@ -274,7 +276,6 @@
     def _():
         imf_copy.start()
 
-    arrived(s.trecv, "t")
 
     def embed_text(i):
         p = s.tpart[rows(i, m * STEP), :] + s.trecv[rows(i), :].astype(F32)
@@ -285,15 +286,11 @@
         s.tsc[rows(i), :] = wide(sc)
         s.txt[y, rows(i, core * TC + zh * WIN), :] = jnp.where(mine, p * sc, 0.0).astype(BF)
 
-    each(WIN // 16, embed_text)
 
     def part(yy, zz, cut=None):
         first, count = (0, WIN) if cut is None else TEXT_PARTS[cut]
         return s.txt.at[yy, pl.ds(pl.multiple_of(core * TC + zz * WIN + first, 16), count)]
 
-    def side(yy, cc):
-        return s.txt.at[yy, pl.ds(pl.multiple_of(cc * TC, 16), TC)]
-
     def send_text(yy, zz, to, cut=None):
         ref = part(yy, zz, cut)
         send(copy(ref, ref, "txt", yy * 4 + zz * 2 + (cut or 0), to))
@@ -302,19 +299,31 @@
         arrived(part(yy, zz, cut), "txt", yy * 4 + zz * 2 + (cut or 0))
 
     def forward_text(zz):
-        text_arrived(y1, zz)
+        text_arrived(y1, zz, 0)
         send_text(y1, zz, ydown, 0)
-        text_arrived(y3, zz)
+        text_arrived(y3, zz, 0)
+        text_arrived(y3, zz, 1)
         send_text(y3, zz, yup, 1)
-
-    def send_twin(yy):
-        send(copy(side(yy, core), side(yy, core), "txtc", yy, twin))
+        send_twin(y3, zz)
+        text_arrived(y1, zz, 1)
+        send_twin(y1, zz)
+
+    def side_part(yy, cc, zz):
+        return s.txt.at[yy, pl.ds(pl.multiple_of(cc * TC + zz * WIN, 16), WIN)]
+
+    def send_twin(yy, zz):
+        send(copy(part(yy, zz), part(yy, zz), "txtc", yy * NZ + zz, twin))
 
     def twin_arrived(yy):
-        arrived(side(yy, oc), "txtc", yy)
-
-    for to in (far, yup, ydown):
-        send_text(y, zh, to)
+        for zz in range(NZ):
+            arrived(side_part(yy, oc, zz), "txtc", yy * NZ + zz)
+
+    for half, (first, count) in enumerate(TEXT_PARTS):
+        arrived(s.trecv.at[pl.ds(first, count)], "t", half)
+        each(count // 16, lambda i, first=first: embed_text(i + first // 16))
+        for to in (far, yup, ydown):
+            send_text(y, zh, to, half)
+    send_twin(y, zh)
 
     def zero(i):
         s.gi[rows(i), :] = jnp.zeros((16, D), F32)
@@ -339,50 +348,51 @@
 
     embed_images(x, 0, own=True)
 
-    text_arrived(y, oz)
-    send_text(y, oz, yup)
-    send_text(y, oz, ydown)
-    send_twin(y)
+    for half in (0, 1):
+        text_arrived(y, oz, half)
+        send_text(y, oz, yup, half)
+        send_text(y, oz, ydown, half)
+    send_twin(y, oz)
     forward_text(zh)
 
-    def unit(yy, half, own=False):
-        r = pl.ds(pl.multiple_of(half * BLOCK, 16), BLOCK)
+    def unit(yy, first, count, own=False):
+        r = pl.ds(first, count)
         texts = s.txt[yy]
         scores = dot(s.img[r, :], texts, NT)
         weights = 0.5 + 0.5 * jnp.tanh((0.5 * LOGIT_SCALE) * scores + 0.5 * LOGIT_BIAS)
         if own:
-            row = lax.broadcasted_iota(jnp.int32, (BLOCK, NC * TC), 0)
-            col = lax.broadcasted_iota(jnp.int32, (BLOCK, NC * TC), 1)
-            first = core * TC + zh * WIN
-            match = (row - col == m * STEP - first) & (col >= first) & (col < first + WIN)
+            row = lax.broadcasted_iota(jnp.int32, (count, NC * TC), 0)
+            col = lax.broadcasted_iota(jnp.int32, (count, NC * TC), 1)
+            at = core * TC + zh * WIN
+            match = (row - col == m * STEP - at) & (col >= at) & (col < at + WIN)
             weights = weights - match.astype(F32)
         weights = weights.astype(BF)
         s.w[yy, r, :] = weights
         s.gi[r, :] += dot(weights, texts, NN)
 
+    twin_arrived(y)
+    unit(y, 0, PAIRS, own=True)
     forward_image(om)
     embed_images(x1, 1)
     embed_images(x3, 2)
     forward_text(oz)
-    send_twin(y1)
-    send_twin(y3)
-    twin_arrived(y)
-    unit(y, 0, own=True)
+    unit(y, PAIRS, 2 * PAIRS)
     twin_arrived(y1)
+    unit(y1, 0, 3 * PAIRS)
     twin_arrived(y3)
-    each(2, lambda i: unit(other(y, 1 + 2 * i, NY), 0))
-    for zz in range(NZ):
+    unit(y3, 0, 3 * PAIRS)
+    for zz in (zh, oz):
         for half in (0, 1):
             text_arrived(y2, zz, half)
-    send_twin(y2)
+        send_twin(y2, zz)
     for half in (0, 1):
         for cut in (0, 1):
             image_arrived(x2, half, cut)
     embed_images(x2, 3)
-    each(3, lambda i: unit(other(y, i + i // 2, NY), 1))
+    each(3, lambda i: unit(other(y, i + i // 2, NY), 3 * PAIRS, PAIRS))
 
     twin_arrived(y2)
-    unit(y2, 1)
+    unit(y2, 2 * PAIRS, 2 * PAIRS)
 
     def cast(at, place, add=None, first=0, count=PAIRS):
         def body(i):
@@ -406,7 +416,7 @@
         send(copy(s.xsend.at[at, r], s.xr.at[at - 1, r], "xr", (at - 1) * 2 + half, to))
 
     image_back(2, 2, 0, xdown)
-    unit(y2, 0)
+    unit(y2, 0, 2 * PAIRS)
     image_back(1, 1, 1, xup)
 
     def text_grad(yy):
@@ -424,8 +434,27 @@
     def back_twin_arrived(yy):
         arrived(s.gtcrecv.at[yy], "gtc", yy)
 
-    text_grad(y2)
+    def columns_of(cc):
+        return s.w[y2, :, pl.ds(cc * TC, TC)]
+
+    @pl.when(core == 0)
+    def _():
+        s.gtcsend[y2] = dot(columns_of(1), s.img[...], TN).astype(BF)
+
+    @pl.when(core == 1)
+    def _():
+        s.gtcsend[y2] = dot(columns_of(0), s.img[...], TN).astype(BF)
+
     send_back_twin(y2)
+
+    @pl.when(core == 0)
+    def _():
+        s.gt[y2] = dot(columns_of(0), s.img[...], TN)
+
+    @pl.when(core == 1)
+    def _():
+        s.gt[y2] = dot(columns_of(1), s.img[...], TN)
+
     text_grad(y1)
     send_back_twin(y1)
     arrived(s.xa, "xa")
@@ -505,8 +534,7 @@
         s.zsend[rows(i), :] = text_sum(rows(i, oz * WIN)).astype(BF)
 
     back_arrived(oz)
-    for half in (0, 1):
-        first, count = TEXT_PARTS[half]
+    for half, (first, count) in enumerate(Z_PARTS):
         each(count // 16, lambda i, first=first: text_far(i + first // 16))
         r = pl.ds(first, count)
         send(copy(s.zsend.at[r], s.zrecv.at[r], "z", half, far))
@@ -530,8 +558,7 @@
         s.tw[m, r, :] = v
         s.sw[m, r, :] = wide(rowsum(v.astype(F32) * p))
 
-    for half in (0, 1):
-        first, count = TEXT_PARTS[half]
+    for half, (first, count) in enumerate(Z_PARTS):
         r = pl.ds(first, count)
         arrived(s.zrecv.at[r], "z", half)
         each(count // 16, lambda i, first=first: text_own(i + first // 16))
@@ -555,101 +582,90 @@
     def _():
         pg_copy.start()
 
-    class Ring:
-        def __init__(self, load, count, bufs, groups, up, down, chunks):
+    class Sum:
+        def __init__(self, load, count, bufs, group, devices, chunks, side):
             self.load, self.count, self.chunks = load, count, chunks
-            self.out, self.ab, self.back = bufs
-            self.groups = groups
-            self.used = pl.ds(0, count * 16)
-            n = self.used
+            self.out, self.back = bufs
+            self.group, self.side = group, side
+            n, cols = self.used, self.cols = pl.ds(0, count * 16), pl.ds(*COLUMNS[side])
             self.copies = [
-                copy(self.out.at[0, 0, n], self.ab.at[0, n], groups[0], 0, up),
-                copy(self.out.at[0, 1, n], self.ab.at[1, n], groups[0], 1, down),
-                copy(self.out.at[1, 1, n], self.back.at[0, 1, n], groups[1], 1, up),
-                copy(self.out.at[2, 0, n], self.back.at[1, 0, n], groups[1], 2, down),
-                copy(self.out.at[1, 0, n], self.back.at[0, 0, n], groups[1], 0, up),
-                copy(self.out.at[2, 1, n], self.back.at[1, 1, n], groups[1], 3, down),
+                copy(self.out.at[at, :, n, cols], self.back.at[at, :, n, cols], group, side * 3 + at, to)
+                for at, to in enumerate(devices)
             ]
 
-        def cast(self, at, chunk, half, add=None):
-            def body(i):
-                v = self.load(chunk, half, i)
-                if add is not None:
-                    v = v + self.ab[add, rows(i), :].astype(F32)
-                self.out[at, half, rows(i), :] = v.astype(BF)
-
-            each(self.count, body)
-
         def begin(self):
+            for at in (1, 0, 2):
+                for half in (0, 1):
+
+                    def body(i, at=at, half=half):
+                        v = self.load(self.chunks[1 + at], half, i)
+                        self.out[at, half, rows(i), self.cols] = v.astype(BF)
+
+                    each(self.count, body)
+                self.copies[at].start()
+
+        def finish(self, store):
+            for at in range(3):
+                arrived(self.back.at[at, :, self.used, self.cols], self.group, self.side * 3 + at)
             for half in (0, 1):
-                self.cast(0, self.chunks[2], half)
-                self.copies[half].start()
-            self.cast(1, self.chunks[1], 1)
-            self.copies[2].start()
-            self.cast(2, self.chunks[3], 0)
-            self.copies[3].start()
-
-        def pass_on(self):
-            arrived(self.ab.at[0, self.used], self.groups[0], 0)
-            self.cast(1, self.chunks[1], 0, add=0)
-            self.copies[4].start()
-            arrived(self.ab.at[1, self.used], self.groups[0], 1)
-            self.cast(2, self.chunks[3], 1, add=1)
-            self.copies[5].start()
-
-        def finish(self, store):
-            for way in (0, 1):
-                for half in (0, 1):
-                    arrived(self.back.at[way, half, self.used], self.groups[1], way * 2 + half)
-            for half in (0, 1):
 
                 def total(i, half=half):
-                    v = self.load(self.chunks[0], half, i) + self.back[0, half, rows(i), :].astype(F32)
-                    store(half, i, v + self.back[1, half, rows(i), :].astype(F32))
+                    v = self.load(self.chunks[0], half, i)
+                    for at in range(3):
+                        v = v + self.back[at, half, rows(i), self.cols].astype(F32)
+                    store(half, i, v)
 
                 each(self.count, total)
             for c in self.copies:
                 c.wait_send()
 
-    def store_first(count):
-        def store(half, i, v):
-            s.h1[rows(i, half * count * 16), :] = v
-
-        return store
-
-    def store_second(half, i, v):
-        s.h2[rows(i, half * XWIN), :] = v
-
-    bufs1, bufs2 = (s.h1send, s.h1ab, s.h1r), (s.h2send, s.h2ab, s.h2r)
+    low, high = (pl.ds(*where) for where in COLUMNS)
+    bufs1, bufs2 = (s.h1send, s.h1r), (s.h2send, s.h2r)
+    along_x, along_y = (xup, dev(xx=x2), xdown), (yup, dev(yy=y2), ydown)
     xs, ys = (x, x1, x2, x3), (y, y1, y2, y3)
-    tall = ZROWS // 16
-    image_first = Ring(
-        lambda c, half, i: s.h[rows(i, c * YROWS + half * ZROWS), :],
-        tall, bufs1, ("h1ab", "h1r"), yup, ydown, ys,
+    tall, short = ZROWS // 16, XWIN // 16
+    x_first = Sum(
+        lambda c, half, i: s.h[rows(lax.rem(i, 3), (half * NY + i // 3) * ZROWS + c * 32), low],
+        XHALF // 16, bufs1, "h1r", along_x, xs, 0,
     )
-    image_second = Ring(
-        lambda c, half, i: s.h1[rows(i, half * ZROWS + c * 32), :],
-        XWIN // 16, bufs2, ("h2ab", "h2r"), xup, xdown, xs,
+    y_second = Sum(
+        lambda c, half, i: s.h1[rows(i, (c * NZ + half) * XWIN), low],
+        short, bufs2, "h2r", along_y, ys, 0,
     )
-    text_first = Ring(
-        lambda c, half, i: s.h[rows(lax.rem(i, 3), (half * NY + i // 3) * ZROWS + c * 32), :],
-        XHALF // 16, bufs1, ("h1ab", "h1r"), xup, xdown, xs,
+    y_first = Sum(
+        lambda c, half, i: s.h[rows(i, c * YROWS + half * ZROWS), high],
+        tall, bufs1, "h1r", along_y, ys, 1,
     )
-    text_second = Ring(
-        lambda c, half, i: s.h1[rows(i, (c * NZ + half) * XWIN), :],
-        XWIN // 16, bufs2, ("h2ab", "h2r"), yup, ydown, ys,
+    x_second = Sum(
+        lambda c, half, i: s.h1[rows(i, half * ZROWS + c * 32), high],
+        short, bufs2, "h2r", along_x, xs, 1,
     )
+
+    def store(to, count, cols):
+        def at(half, i, v):
+            to[rows(i, half * count * 16), cols] = v
+
+        return at
 
     @pl.when(core == 0)
     def _():
         arrived(s.imft, "imft")
         arrived(s.pgt, "pgt")
         s.h[...] = dot(s.imf[...], s.pg[...], TN) + dot(s.imft[...], s.pgt[...], TN)
-        image_first.begin()
-        image_first.pass_on()
-
-    for half in (0, 1):
-        arrived(s.tw.at[om, pl.ds(*TEXT_PARTS[half])], "tw", half)
+        x_first.begin()
+        y_first.begin()
+
+    s.gip[...] = dot(s.pg[...], s.iht[...], NN)
+
+    def image_out(i):
+        s.gsend[rows(i), :] = pick(s.gip[rows(i), :], om).astype(BF)
+
+    each(PAIRS // 16, image_out)
+
+    for half, where in enumerate(Z_PARTS):
+        arrived(s.tw.at[om, pl.ds(*where)], "tw", half)
+
+    send(copy(s.gsend, s.grecv, "g", 0, mate))
 
     def merge(i):
         lo, hi = jnp.minimum(i, 6), jnp.maximum(i - 6, 0)
@@ -668,24 +684,14 @@
         arrived(s.nhbt, "nhbt")
         arrived(s.tpgt, "tpgt")
         s.h[...] = dot(s.tpg[...], s.nhb[...], TN) + dot(s.tpgt[...], s.nhbt[...], TN)
-        text_first.begin()
-
-    s.gip[...] = dot(s.pg[...], s.iht[...], NN)
-
-    def image_out(i):
-        s.gsend[rows(i), :] = pick(s.gip[rows(i), :], om).astype(BF)
-
-    each(PAIRS // 16, image_out)
-
-    send(copy(s.gsend, s.grecv, "g", 0, mate))
-
-    @pl.when(core == 1)
-    def _():
-        text_first.pass_on()
+        x_first.begin()
+        y_first.begin()
+
+
+    g_txt[...] = dot(s.tpg[...], s.th[...], NT)
 
     arrived(s.sw.at[om], "sw")
     arrived(s.u.at[om], "u")
-    g_txt[...] = dot(s.tpg[...], s.th[...], NT)
 
     def text_input(i):
         r = rows(i)
@@ -698,6 +704,29 @@
 
     each(PAIRS // 16, text_input)
 
+    x_first.finish(store(s.h1, XHALF // 16, low))
+    y_second.begin()
+    y_first.finish(store(s.h1, tall, high))
+    x_second.begin()
+    y_second.finish(store(s.h2, short, low))
+    x_second.finish(store(s.h2, short, high))
+
+    @pl.when(core == 0)
+    def _():
+        nhb_copy.wait_send()
+        tpg_copy.wait_send()
+
+    @pl.when(core == 1)
+    def _():
+        imf_copy.wait_send()
+        pg_copy.wait_send()
+
+    def head_far(i):
+        s.h3send[rows(i), :] = s.h2[rows(i, oz * XWIN), :].astype(BF)
+
+    each(XWIN // 16, head_far)
+    send(copy(s.h3send, s.h3recv, "h3", 0, dev(zz=oz)))
+
     arrived(s.grecv, "g")
 
     def image_input(i):
@@ -706,29 +735,6 @@
 
     each(PAIRS // 16, image_input)
 
-    @pl.when(core == 0)
-    def _():
-        image_first.finish(store_first(tall))
-        image_second.begin()
-        image_second.pass_on()
-        image_second.finish(store_second)
-        nhb_copy.wait_send()
-        tpg_copy.wait_send()
-
-    @pl.when(core == 1)
-    def _():
-        text_first.finish(store_first(XHALF // 16))
-        text_second.begin()
-        text_second.pass_on()
-        text_second.finish(store_second)
-        imf_copy.wait_send()
-        pg_copy.wait_send()
-
-    def head_far(i):
-        s.h3send[rows(i), :] = s.h2[rows(i, oz * XWIN), :].astype(BF)
-
-    each(XWIN // 16, head_far)
-    send(copy(s.h3send, s.h3recv, "h3", 0, dev(zz=oz)))
     arrived(s.h3recv, "h3")
 
     def head_near(i):

time: 121 us -> 114 us (0.942)
  Pallas kernels: 115 us -> 108 us
    pallas_call x1, Pallas kernels: 115 us -> 108 us  [per_device(): pl.pallas_call(kernel, out_shape=(jax.ShapeDtypeStruct((PAIRS, HALF), F32...]
where the time goes in v2:
time: 114 us
  Pallas kernels  108 us (95%)
  local copies, waits for them, and re-layouts  4.81 us (4%)
    pallas_call x1, Pallas kernels, per_device(): pl.pallas_call(kernel, out_shape=(jax.ShapeDtypeStruct((PAIRS, HALF), F32...  108 us
    unnamed x8, local copies, waits for them, and re-layouts  4.81 us

profile of v2, /device:TPU:1, one launch (start us, length us, event | category | flops | bytes accessed | tf_op | source)
XLA Modules:
  0.0 113.7 jit_solution(18361607159876580925)
XLA Ops:
  0.6 108.2 %shard_map.75 = (f32[208,576]{1,0:T(8,128)}, f32[18,576]{1,0:T(8,128)}, f32[208,576]{1,0:T(8,128)}, f32[18,576]{1,0:T(8,128)}) custom-call(bf16[208,1152]{1,0:T(8,128)(2,1)} %img_feat.1, bf16[576,1152]{1,0:T(8,128)(2,1)} %bitcast.3, bf16[208,1152]{1,0:T(8,128)(2,1)} %txt_feat.1, bf16[576,1152]{1,0:T(8,128)(2,1)} %txt_head.1), custom_call_target="tpu_custom_call" | custom-call | flops 14000000000 | bytes 5000000 | tf_op jit(solution)/shard_map/pallas_call | solution.py:758
  108.9 0.0 copy-start
  108.9 0.0 copy-start.1
  108.9 1.9 %copy.12 = f32[208,576]{1,0:T(8,128)} copy(f32[208,576]{1,0:T(8,128)} %get-tuple-element.16) | data formatting | bytes 958464
  110.8 1.5 %copy.13 = f32[18,576]{1,0:T(8,128)} copy(f32[18,576]{1,0:T(8,128)} %get-tuple-element.17) | data formatting | bytes 82944
  112.3 0.0 copy-done
  112.3 0.8 copy.14
  113.1 0.0 copy-done.1
  113.1 0.6 copy.15
Async XLA Ops:
  108.9 3.4 %copy-start = (f32[208,576]{1,0:T(8,128)S(1)}, f32[208,576]{1,0:T(8,128)}, u32[]{:S(2)}) copy-start(f32[208,576]{1,0:T(8,128)} %get-tuple-element.18) | copy-start | bytes 1437700
  108.9 4.2 %copy-start.1 = (f32[18,576]{1,0:T(8,128)S(1)}, f32[18,576]{1,0:T(8,128)}, u32[]{:S(2)}) copy-start(f32[18,576]{1,0:T(8,128)} %get-tuple-element.11) | copy-start | bytes 124420

commit v3 on v2

--- a/solution.py
+++ b/solution.py
@@ -213,17 +213,13 @@
 
     loads[0].wait()
 
-    def norm(i):
-        r = rows(i)
-        t = s.tf[r, :].astype(F32)
-        c = t - rowsum(t) * (1.0 / D)
-        rs = lax.rsqrt(rowsum(c * c) * (1.0 / D) + NORM_EPS)
-        half = pick(c * rs, m)
-        s.nhf[r, :] = half
-        s.nhb[r, :] = half.astype(BF)
-        s.rs[r, :] = wide(rs)
-
-    each(PAIRS // 16, norm)
+    t = s.tf[...].astype(F32)
+    t = t - rowsum(t) * (1.0 / D)
+    rs = lax.rsqrt(rowsum(t * t) * (1.0 / D) + NORM_EPS)
+    half = pick(t * rs, m)
+    s.nhf[...] = half
+    s.nhb[...] = half.astype(BF)
+    s.rs[...] = wide(rs)
     loads[1].wait()
     s.tpart[...] = dot(s.nhb[...], s.th[...], NN)
 
@@ -277,15 +273,21 @@
         imf_copy.start()
 
 
-    def embed_text(i):
-        p = s.tpart[rows(i, m * STEP), :] + s.trecv[rows(i), :].astype(F32)
+    def own_rows(first, count):
+        row = m * STEP + first + lax.broadcasted_iota(jnp.int32, (count, 1), 0)
+        return (row >= m * OWN) & (row < m * OWN + OWN)
+
+    def at16(first, count):
+        return pl.ds(pl.multiple_of(first, 16), count)
+
+    def embed_text(first, count):
+        r = pl.ds(first, count)
+        p = s.tpart[at16(m * STEP + first, count), :] + s.trecv[r, :].astype(F32)
         sc = lax.rsqrt(rowsum(p * p) + NORM_EPS)
-        row = m * STEP + i * 16 + lax.broadcasted_iota(jnp.int32, (16, 1), 0)
-        mine = (row >= m * OWN) & (row < m * OWN + OWN)
-        s.tproj[rows(i), :] = p
-        s.tsc[rows(i), :] = wide(sc)
-        s.txt[y, rows(i, core * TC + zh * WIN), :] = jnp.where(mine, p * sc, 0.0).astype(BF)
-
+        s.tproj[r, :] = p
+        s.tsc[r, :] = wide(sc)
+        emb = jnp.where(own_rows(first, count), p * sc, 0.0).astype(BF)
+        s.txt[y, at16(core * TC + zh * WIN + first, count), :] = emb
 
     def part(yy, zz, cut=None):
         first, count = (0, WIN) if cut is None else TEXT_PARTS[cut]
@@ -320,7 +322,7 @@
 
     for half, (first, count) in enumerate(TEXT_PARTS):
         arrived(s.trecv.at[pl.ds(first, count)], "t", half)
-        each(count // 16, lambda i, first=first: embed_text(i + first // 16))
+        embed_text(first, count)
         for to in (far, yup, ydown):
             send_text(y, zh, to, half)
     send_twin(y, zh)
@@ -336,15 +338,11 @@
     send_image(x, om, xdown)
 
     def embed_images(xx, at, own=False):
-        def embed(i):
-            r = rows(i)
-            p = jnp.concatenate([s.imh[xx, 0, r, :].astype(F32), s.imh[xx, 1, r, :].astype(F32)], axis=1)
-            sc = lax.rsqrt(rowsum(p * p) + NORM_EPS)
-            if own:
-                s.isc[r, :] = wide(sc)
-            s.img[rows(i, at * PAIRS), :] = (p * sc).astype(BF)
-
-        each(PAIRS // 16, embed)
+        p = jnp.concatenate([s.imh[xx, 0].astype(F32), s.imh[xx, 1].astype(F32)], axis=1)
+        sc = lax.rsqrt(rowsum(p * p) + NORM_EPS)
+        if own:
+            s.isc[...] = wide(sc)
+        s.img[pl.ds(at * PAIRS, PAIRS), :] = (p * sc).astype(BF)
 
     embed_images(x, 0, own=True)
 
@@ -370,13 +368,12 @@
         s.w[yy, r, :] = weights
         s.gi[r, :] += dot(weights, texts, NN)
 
-    twin_arrived(y)
-    unit(y, 0, PAIRS, own=True)
     forward_image(om)
+    forward_text(oz)
     embed_images(x1, 1)
     embed_images(x3, 2)
-    forward_text(oz)
-    unit(y, PAIRS, 2 * PAIRS)
+    twin_arrived(y)
+    unit(y, 0, 3 * PAIRS, own=True)
     twin_arrived(y1)
     unit(y1, 0, 3 * PAIRS)
     twin_arrived(y3)
@@ -457,10 +454,6 @@
 
     text_grad(y1)
     send_back_twin(y1)
-    arrived(s.xa, "xa")
-    image_back(1, 1, 0, xup, add=s.xa)
-    arrived(s.xb, "xb")
-    image_back(2, 2, 1, xdown, add=s.xb)
     back_twin_arrived(y2)
 
     def text_back(at, yy, zz, half, dst, group, index, to, add=None):
@@ -491,6 +484,10 @@
     back_twin_arrived(y3)
     for zz in (oz, zh):
         text_back_to(2, y3, zz, 0, ydown)
+    arrived(s.xa, "xa")
+    image_back(1, 1, 0, xup, add=s.xa)
+    arrived(s.xb, "xb")
+    image_back(2, 2, 1, xdown, add=s.xb)
     text_grad(y)
     send_back_twin(y)
     for zz in (oz, zh):
@@ -504,18 +501,12 @@
         for half in (0, 1):
             arrived(s.xr.at[way, pl.ds(*IMAGE_PARTS[half])], "xr", way * 2 + half)
 
-    def projection(r):
-        return jnp.concatenate([s.imh[x, 0, r, :].astype(F32), s.imh[x, 1, r, :].astype(F32)], axis=1)
-
-    def image_sum(i):
-        r = rows(i)
-        g = s.gi[rows(i), :] + s.xr[0, r, :].astype(F32) + s.xr[1, r, :].astype(F32)
-        g = LOGIT_SCALE * g
-        s.dots[m, r, :] = wide(rowsum(g * projection(r)))
-        s.ghalf[r, :] = pick(g, m)
-        s.izsend[r, :] = pick(g, om).astype(BF)
-
-    each(PAIRS // 16, image_sum)
+    g = s.gi[pl.ds(0, PAIRS), :] + s.xr[0].astype(F32) + s.xr[1].astype(F32)
+    g = LOGIT_SCALE * g
+    p = jnp.concatenate([s.imh[x, 0].astype(F32), s.imh[x, 1].astype(F32)], axis=1)
+    s.dots[m] = wide(rowsum(g * p))
+    s.ghalf[...] = pick(g, m)
+    s.izsend[...] = pick(g, om).astype(BF)
     send(copy(s.dots.at[m], s.dots.at[m], "dots", 0, mate))
     send(copy(s.izsend, s.izrecv, "iz", 0, mate))
 
@@ -546,37 +537,31 @@
     each(WIN // 16, text_near)
 
 
-    def text_own(i):
-        r = rows(i)
+    def text_own(first, count):
+        r = pl.ds(first, count)
         g = LOGIT_SCALE * (s.gown[r, :] + s.zrecv[r, :].astype(F32))
         p = s.tproj[r, :]
         sc = s.tsc[r, :][:, :1]
         v = sc * g - (sc * sc * sc) * p * rowsum(p * g)
-        row = m * STEP + i * 16 + lax.broadcasted_iota(jnp.int32, (16, 1), 0)
-        mine = (row >= m * OWN) & (row < m * OWN + OWN)
-        v = jnp.where(mine, v, 0.0).astype(BF)
+        v = jnp.where(own_rows(first, count), v, 0.0).astype(BF)
         s.tw[m, r, :] = v
         s.sw[m, r, :] = wide(rowsum(v.astype(F32) * p))
 
     for half, (first, count) in enumerate(Z_PARTS):
         r = pl.ds(first, count)
         arrived(s.zrecv.at[r], "z", half)
-        each(count // 16, lambda i, first=first: text_own(i + first // 16))
+        text_own(first, count)
         send(copy(s.tw.at[m, r], s.tw.at[m, r], "tw", half, mate))
     send(copy(s.sw.at[m], s.sw.at[m], "sw", 0, mate))
 
     arrived(s.dots.at[om], "dots")
     arrived(s.izrecv, "iz")
 
-    def image_grad(i):
-        r = rows(i)
-        g = s.ghalf[r, :] + s.izrecv[r, :].astype(F32)
-        sc = s.isc[r, :][:, :1]
-        total = (s.dots[0, r, :] + s.dots[1, r, :])[:, :1]
-        p = s.imh[x, m, r, :].astype(F32)
-        s.pg[r, :] = (sc * g - (sc * sc * sc) * p * total).astype(BF)
-
-    each(PAIRS // 16, image_grad)
+    g = s.ghalf[...] + s.izrecv[...].astype(F32)
+    sc = s.isc[...][:, :1]
+    total = (s.dots[0] + s.dots[1])[:, :1]
+    p = s.imh[x, m].astype(F32)
+    s.pg[...] = (sc * g - (sc * sc * sc) * p * total).astype(BF)
 
     @pl.when(core == 1)
     def _():
@@ -667,13 +652,12 @@
 
     send(copy(s.gsend, s.grecv, "g", 0, mate))
 
-    def merge(i):
-        lo, hi = jnp.minimum(i, 6), jnp.maximum(i - 6, 0)
-        v = jnp.where(i <= 6, s.tw[0, rows(lo), :].astype(F32), 0.0)
-        v = v + jnp.where(i >= 6, s.tw[1, rows(hi), :].astype(F32), 0.0)
-        s.tpg[rows(i), :] = v.astype(BF)
-
-    each(PAIRS // 16, merge)
+    def merged(a, b):
+        a, b = a.astype(F32), b.astype(F32)
+        both = a[STEP:, :] + b[: WIN - STEP, :]
+        return jnp.concatenate([a[:STEP, :], both, b[WIN - STEP :, :]], axis=0)
+
+    s.tpg[...] = merged(s.tw[0], s.tw[1]).astype(BF)
 
     @pl.when(core == 0)
     def _():
@@ -693,16 +677,10 @@
     arrived(s.sw.at[om], "sw")
     arrived(s.u.at[om], "u")
 
-    def text_input(i):
-        r = rows(i)
-        u = (s.u[0] + s.u[1])[:1, :]
-        first = rowsum(s.tpg[r, :].astype(F32) * u) * (1.0 / D)
-        lo, hi = jnp.minimum(i, 6), jnp.maximum(i - 6, 0)
-        second = jnp.where(i <= 6, s.sw[0, rows(lo), :], 0.0) + jnp.where(i >= 6, s.sw[1, rows(hi), :], 0.0)
-        second = second[:, :1] * (1.0 / D)
-        g_txt[r, :] = s.rs[r, :][:, :1] * (g_txt[r, :] - first - s.nhf[r, :] * second)
-
-    each(PAIRS // 16, text_input)
+    u = (s.u[0] + s.u[1])[:1, :]
+    mean = rowsum(s.tpg[...].astype(F32) * u) * (1.0 / D)
+    product = merged(s.sw[0], s.sw[1])[:, :1] * (1.0 / D)
+    g_txt[...] = s.rs[...][:, :1] * (g_txt[...] - mean - s.nhf[...] * product)
 
     x_first.finish(store(s.h1, XHALF // 16, low))
     y_second.begin()

time: 114 us -> 104 us (0.912)
  Pallas kernels: 108 us -> 98.3 us
    pallas_call x1, Pallas kernels: 108 us -> 98.3 us  [per_device(): pl.pallas_call(kernel, out_shape=(jax.ShapeDtypeStruct((PAIRS, HALF), F32...]
where the time goes in v3:
time: 104 us
  Pallas kernels  98.3 us (95%)
  local copies, waits for them, and re-layouts  4.81 us (5%)
    pallas_call x1, Pallas kernels, per_device(): pl.pallas_call(kernel, out_shape=(jax.ShapeDtypeStruct((PAIRS, HALF), F32...  98.3 us
    unnamed x8, local copies, waits for them, and re-layouts  4.81 us

profile of v3, /device:TPU:1, one launch (start us, length us, event | category | flops | bytes accessed | tf_op | source)
XLA Modules:
  0.0 103.8 jit_solution(2013521830591816758)
XLA Ops:
  0.6 98.3 %shard_map.75 = (f32[208,576]{1,0:T(8,128)}, f32[18,576]{1,0:T(8,128)}, f32[208,576]{1,0:T(8,128)}, f32[18,576]{1,0:T(8,128)}) custom-call(bf16[208,1152]{1,0:T(8,128)(2,1)} %img_feat.1, bf16[576,1152]{1,0:T(8,128)(2,1)} %bitcast.3, bf16[208,1152]{1,0:T(8,128)(2,1)} %txt_feat.1, bf16[576,1152]{1,0:T(8,128)(2,1)} %txt_head.1), custom_call_target="tpu_custom_call" | custom-call | flops 14000000000 | bytes 5000000 | tf_op jit(solution)/shard_map/pallas_call | solution.py:736
  99.0 0.0 copy-start
  99.0 0.0 copy-start.1
  99.0 1.9 %copy.12 = f32[208,576]{1,0:T(8,128)} copy(f32[208,576]{1,0:T(8,128)} %get-tuple-element.16) | data formatting | bytes 958464
  100.9 1.5 %copy.13 = f32[18,576]{1,0:T(8,128)} copy(f32[18,576]{1,0:T(8,128)} %get-tuple-element.17) | data formatting | bytes 82944
  102.4 0.0 copy-done
  102.4 0.8 copy.14
  103.2 0.0 copy-done.1
  103.2 0.6 copy.15
Async XLA Ops:
  99.0 3.4 %copy-start = (f32[208,576]{1,0:T(8,128)S(1)}, f32[208,576]{1,0:T(8,128)}, u32[]{:S(2)}) copy-start(f32[208,576]{1,0:T(8,128)} %get-tuple-element.18) | copy-start | bytes 1437700
  99.0 4.2 %copy-start.1 = (f32[18,576]{1,0:T(8,128)S(1)}, f32[18,576]{1,0:T(8,128)}, u32[]{:S(2)}) copy-start(f32[18,576]{1,0:T(8,128)} %get-tuple-element.11) | copy-start | bytes 124420

commit v4 on v3

--- a/solution.py
+++ b/solution.py
@@ -92,7 +92,7 @@
     "nhbt": ((PAIRS, HALF), BF),
     "pgt": ((PAIRS, HALF), BF),
     "tpgt": ((PAIRS, D), BF),
-    "h": ((D, HALF), F32),
+    "h": ((NY * NZ, ZROWS, HALF), F32),
     "h1send": ((3, 2, XHALF, HALF), BF),
     "h1r": ((3, 2, XHALF, HALF), BF),
     "h1": ((2 * XHALF, HALF), F32),
@@ -392,13 +392,10 @@
     unit(y2, 2 * PAIRS, 2 * PAIRS)
 
     def cast(at, place, add=None, first=0, count=PAIRS):
-        def body(i):
-            v = s.gi[rows(i, place * PAIRS + first), :]
-            if add is not None:
-                v = v + add[rows(i), :].astype(F32)
-            s.xsend[at, rows(i, first), :] = v.astype(BF)
-
-        each(count // 16, body)
+        v = s.gi[pl.ds(place * PAIRS + first, count), :]
+        if add is not None:
+            v = v + add[...].astype(F32)
+        s.xsend[at, pl.ds(first, count), :] = v.astype(BF)
 
     for half in (0, 1):
         first, count = IMAGE_PARTS[half]
@@ -459,15 +456,11 @@
     def text_back(at, yy, zz, half, dst, group, index, to, add=None):
         first, count = TEXT_PARTS[half]
 
-        def body(i):
-            r = rows(i, zz * WIN + first)
-            v = s.gt[yy, r, :] + s.gtcrecv[yy, r, :].astype(F32)
-            if add is not None:
-                v = v + add[zz, rows(i), :].astype(F32)
-            s.ysend[at, r, :] = v.astype(BF)
-
-        each(count // 16, body)
-        r = pl.ds(pl.multiple_of(zz * WIN + first, 16), count)
+        r = at16(zz * WIN + first, count)
+        v = s.gt[yy, r, :] + s.gtcrecv[yy, r, :].astype(F32)
+        if add is not None:
+            v = v + add[zz].astype(F32)
+        s.ysend[at, r, :] = v.astype(BF)
         send(copy(s.ysend.at[at, r], dst(r), group, index, to))
 
     def text_back_to(at, yy, zz, half, to, add=None):
@@ -521,20 +514,14 @@
         g = s.gt[y, r, :] + s.gtcrecv[y, r, :].astype(F32)
         return g + s.yr[0, r, :].astype(F32) + s.yr[1, r, :].astype(F32)
 
-    def text_far(i):
-        s.zsend[rows(i), :] = text_sum(rows(i, oz * WIN)).astype(BF)
-
     back_arrived(oz)
     for half, (first, count) in enumerate(Z_PARTS):
-        each(count // 16, lambda i, first=first: text_far(i + first // 16))
         r = pl.ds(first, count)
+        s.zsend[r, :] = text_sum(at16(oz * WIN + first, count)).astype(BF)
         send(copy(s.zsend.at[r], s.zrecv.at[r], "z", half, far))
     back_arrived(zh)
 
-    def text_near(i):
-        s.gown[rows(i), :] = text_sum(rows(i, zh * WIN))
-
-    each(WIN // 16, text_near)
+    s.gown[...] = text_sum(at16(zh * WIN, WIN))
 
 
     def text_own(first, count):
@@ -569,10 +556,10 @@
 
     class Sum:
         def __init__(self, load, count, bufs, group, devices, chunks, side):
-            self.load, self.count, self.chunks = load, count, chunks
+            self.load, self.chunks = load, chunks
             self.out, self.back = bufs
             self.group, self.side = group, side
-            n, cols = self.used, self.cols = pl.ds(0, count * 16), pl.ds(*COLUMNS[side])
+            n, cols = self.used, self.cols = pl.ds(0, count), pl.ds(*COLUMNS[side])
             self.copies = [
                 copy(self.out.at[at, :, n, cols], self.back.at[at, :, n, cols], group, side * 3 + at, to)
                 for at, to in enumerate(devices)
@@ -581,26 +568,17 @@
         def begin(self):
             for at in (1, 0, 2):
                 for half in (0, 1):
-
-                    def body(i, at=at, half=half):
-                        v = self.load(self.chunks[1 + at], half, i)
-                        self.out[at, half, rows(i), self.cols] = v.astype(BF)
-
-                    each(self.count, body)
+                    self.out[at, half, self.used, self.cols] = self.load(self.chunks[1 + at], half).astype(BF)
                 self.copies[at].start()
 
         def finish(self, store):
             for at in range(3):
                 arrived(self.back.at[at, :, self.used, self.cols], self.group, self.side * 3 + at)
             for half in (0, 1):
-
-                def total(i, half=half):
-                    v = self.load(self.chunks[0], half, i)
-                    for at in range(3):
-                        v = v + self.back[at, half, rows(i), self.cols].astype(F32)
-                    store(half, i, v)
-
-                each(self.count, total)
+                v = self.load(self.chunks[0], half)
+                for at in range(3):
+                    v = v + self.back[at, half, self.used, self.cols].astype(F32)
+                store(half, v)
             for c in self.copies:
                 c.wait_send()
 
@@ -608,27 +586,23 @@
     bufs1, bufs2 = (s.h1send, s.h1r), (s.h2send, s.h2r)
     along_x, along_y = (xup, dev(xx=x2), xdown), (yup, dev(yy=y2), ydown)
     xs, ys = (x, x1, x2, x3), (y, y1, y2, y3)
-    tall, short = ZROWS // 16, XWIN // 16
     x_first = Sum(
-        lambda c, half, i: s.h[rows(lax.rem(i, 3), (half * NY + i // 3) * ZROWS + c * 32), low],
-        XHALF // 16, bufs1, "h1r", along_x, xs, 0,
+        lambda c, half: s.h[pl.ds(half * NY, NY), at16(c * 32, XWIN), low].reshape(XHALF, COLUMNS[0][1]),
+        XHALF, bufs1, "h1r", along_x, xs, 0,
     )
     y_second = Sum(
-        lambda c, half, i: s.h1[rows(i, (c * NZ + half) * XWIN), low],
-        short, bufs2, "h2r", along_y, ys, 0,
+        lambda c, half: s.h1[at16((c * NZ + half) * XWIN, XWIN), low],
+        XWIN, bufs2, "h2r", along_y, ys, 0,
     )
-    y_first = Sum(
-        lambda c, half, i: s.h[rows(i, c * YROWS + half * ZROWS), high],
-        tall, bufs1, "h1r", along_y, ys, 1,
+    y_first = Sum(lambda c, half: s.h[c * NZ + half, :, high], ZROWS, bufs1, "h1r", along_y, ys, 1)
+    x_second = Sum(
+        lambda c, half: s.h1[at16(half * ZROWS + c * 32, XWIN), high],
+        XWIN, bufs2, "h2r", along_x, xs, 1,
     )
-    x_second = Sum(
-        lambda c, half, i: s.h1[rows(i, half * ZROWS + c * 32), high],
-        short, bufs2, "h2r", along_x, xs, 1,
-    )
 
     def store(to, count, cols):
-        def at(half, i, v):
-            to[rows(i, half * count * 16), cols] = v
+        def at(half, v):
+            to[pl.ds(half * count, count), cols] = v
 
         return at
 
@@ -636,7 +610,8 @@
     def _():
         arrived(s.imft, "imft")
         arrived(s.pgt, "pgt")
-        s.h[...] = dot(s.imf[...], s.pg[...], TN) + dot(s.imft[...], s.pgt[...], TN)
+        h = dot(s.imf[...], s.pg[...], TN) + dot(s.imft[...], s.pgt[...], TN)
+        s.h[...] = h.reshape(s.h.shape)
         x_first.begin()
         y_first.begin()
 
@@ -667,7 +642,8 @@
     def _():
         arrived(s.nhbt, "nhbt")
         arrived(s.tpgt, "tpgt")
-        s.h[...] = dot(s.tpg[...], s.nhb[...], TN) + dot(s.tpgt[...], s.nhbt[...], TN)
+        h = dot(s.tpg[...], s.nhb[...], TN) + dot(s.tpgt[...], s.nhbt[...], TN)
+        s.h[...] = h.reshape(s.h.shape)
         x_first.begin()
         y_first.begin()
 
@@ -682,12 +658,12 @@
     product = merged(s.sw[0], s.sw[1])[:, :1] * (1.0 / D)
     g_txt[...] = s.rs[...][:, :1] * (g_txt[...] - mean - s.nhf[...] * product)
 
-    x_first.finish(store(s.h1, XHALF // 16, low))
+    x_first.finish(store(s.h1, XHALF, low))
     y_second.begin()
-    y_first.finish(store(s.h1, tall, high))
+    y_first.finish(store(s.h1, ZROWS, high))
     x_second.begin()
-    y_second.finish(store(s.h2, short, low))
-    x_second.finish(store(s.h2, short, high))
+    y_second.finish(store(s.h2, XWIN, low))
+    x_second.finish(store(s.h2, XWIN, high))
 
     @pl.when(core == 0)
     def _():

time: 104 us -> 103 us (level)
  Pallas kernels: 98.3 us -> 96.9 us
    pallas_call x1, Pallas kernels: 98.3 us -> 96.9 us  [per_device(): pl.pallas_call(kernel, out_shape=(jax.ShapeDtypeStruct((PAIRS, HALF), F32...]
where the time goes in v4:
time: 103 us; the launch traced here: 102 us
  Pallas kernels  96.9 us (94%)
  local copies, waits for them, and re-layouts  4.81 us (5%)
    pallas_call x1, Pallas kernels, per_device(): pl.pallas_call(kernel, out_shape=(jax.ShapeDtypeStruct((PAIRS, HALF), F32...  96.9 us
    unnamed x8, local copies, waits for them, and re-layouts  4.81 us

profile of v4, /device:TPU:1, one launch (start us, length us, event | category | flops | bytes accessed | tf_op | source)
XLA Modules:
  0.0 102.4 jit_solution(12274340464424749021)
XLA Ops:
  0.6 96.9 %shard_map.75 = (f32[208,576]{1,0:T(8,128)}, f32[18,576]{1,0:T(8,128)}, f32[208,576]{1,0:T(8,128)}, f32[18,576]{1,0:T(8,128)}) custom-call(bf16[208,1152]{1,0:T(8,128)(2,1)} %img_feat.1, bf16[576,1152]{1,0:T(8,128)(2,1)} %bitcast.3, bf16[208,1152]{1,0:T(8,128)(2,1)} %txt_feat.1, bf16[576,1152]{1,0:T(8,128)(2,1)} %txt_head.1), custom_call_target="tpu_custom_call" | custom-call | flops 14000000000 | bytes 5000000 | tf_op jit(solution)/shard_map/pallas_call | solution.py:712
  97.6 0.0 copy-start
  97.6 0.0 copy-start.1
  97.6 1.9 %copy.12 = f32[208,576]{1,0:T(8,128)} copy(f32[208,576]{1,0:T(8,128)} %get-tuple-element.16) | data formatting | bytes 958464
  99.5 1.5 %copy.13 = f32[18,576]{1,0:T(8,128)} copy(f32[18,576]{1,0:T(8,128)} %get-tuple-element.17) | data formatting | bytes 82944
  101.0 0.0 copy-done
  101.0 0.8 copy.14
  101.8 0.0 copy-done.1
  101.8 0.6 copy.15
Async XLA Ops:
  97.6 3.4 %copy-start = (f32[208,576]{1,0:T(8,128)S(1)}, f32[208,576]{1,0:T(8,128)}, u32[]{:S(2)}) copy-start(f32[208,576]{1,0:T(8,128)} %get-tuple-element.18) | copy-start | bytes 1437700
  97.6 4.2 %copy-start.1 = (f32[18,576]{1,0:T(8,128)S(1)}, f32[18,576]{1,0:T(8,128)}, u32[]{:S(2)}) copy-start(f32[18,576]{1,0:T(8,128)} %get-tuple-element.11) | copy-start | bytes 124420

commit v5 on v4

--- a/solution.py
+++ b/solution.py
@@ -223,10 +223,7 @@
     loads[1].wait()
     s.tpart[...] = dot(s.nhb[...], s.th[...], NN)
 
-    def tosend(i):
-        s.tsend[rows(i), :] = s.tpart[rows(i, om * STEP), :].astype(BF)
-
-    each(WIN // 16, tosend)
+    s.tsend[...] = s.tpart[pl.ds(pl.multiple_of(om * STEP, 16), WIN), :].astype(BF)
     pl.semaphore_wait(barrier, len(friends))
     for half, where in enumerate(TEXT_PARTS):
         r = pl.ds(*where)
@@ -416,11 +413,8 @@
     def text_grad(yy):
         s.gtall[...] = dot(s.w[yy], s.img[...], TN)
 
-        def out(i):
-            s.gtcsend[yy, rows(i), :] = s.gtall[rows(i, oc * TC), :].astype(BF)
-            s.gt[yy, rows(i), :] = s.gtall[rows(i, core * TC), :]
-
-        each(TC // 16, out)
+        s.gtcsend[yy] = s.gtall[at16(oc * TC, TC), :].astype(BF)
+        s.gt[yy] = s.gtall[at16(core * TC, TC), :]
 
     def send_back_twin(yy):
         send(copy(s.gtcsend.at[yy], s.gtcrecv.at[yy], "gtc", yy, twin))
@@ -617,11 +611,7 @@
 
     s.gip[...] = dot(s.pg[...], s.iht[...], NN)
 
-    def image_out(i):
-        s.gsend[rows(i), :] = pick(s.gip[rows(i), :], om).astype(BF)
-
-    each(PAIRS // 16, image_out)
-
+    s.gsend[...] = pick(s.gip[...], om).astype(BF)
     for half, where in enumerate(Z_PARTS):
         arrived(s.tw.at[om, pl.ds(*where)], "tw", half)
 

time: 103 us -> 103 us (level)
  no operation moved by 1% of the time
where the time goes in v5:
time: 103 us
  Pallas kernels  97.1 us (94%)
  local copies, waits for them, and re-layouts  4.81 us (5%)
    pallas_call x1, Pallas kernels, per_device(): pl.pallas_call(kernel, out_shape=(jax.ShapeDtypeStruct((PAIRS, HALF), F32...  97.1 us
    unnamed x8, local copies, waits for them, and re-layouts  4.81 us

profile of v5, /device:TPU:1, one launch (start us, length us, event | category | flops | bytes accessed | tf_op | source)
XLA Modules:
  0.0 102.6 jit_solution(17785855924592759101)
XLA Ops:
  0.6 97.1 %shard_map.75 = (f32[208,576]{1,0:T(8,128)}, f32[18,576]{1,0:T(8,128)}, f32[208,576]{1,0:T(8,128)}, f32[18,576]{1,0:T(8,128)}) custom-call(bf16[208,1152]{1,0:T(8,128)(2,1)} %img_feat.1, bf16[576,1152]{1,0:T(8,128)(2,1)} %bitcast.3, bf16[208,1152]{1,0:T(8,128)(2,1)} %txt_feat.1, bf16[576,1152]{1,0:T(8,128)(2,1)} %txt_head.1), custom_call_target="tpu_custom_call" | custom-call | flops 14000000000 | bytes 5000000 | tf_op jit(solution)/shard_map/pallas_call | solution.py:702
  97.7 0.0 copy-start
  97.7 0.0 copy-start.1
  97.7 1.9 %copy.12 = f32[208,576]{1,0:T(8,128)} copy(f32[208,576]{1,0:T(8,128)} %get-tuple-element.16) | data formatting | bytes 958464
  99.7 1.5 %copy.13 = f32[18,576]{1,0:T(8,128)} copy(f32[18,576]{1,0:T(8,128)} %get-tuple-element.17) | data formatting | bytes 82944
  101.1 0.0 copy-done
  101.1 0.8 copy.14
  101.9 0.0 copy-done.1
  101.9 0.6 copy.15
Async XLA Ops:
  97.7 3.4 %copy-start = (f32[208,576]{1,0:T(8,128)S(1)}, f32[208,576]{1,0:T(8,128)}, u32[]{:S(2)}) copy-start(f32[208,576]{1,0:T(8,128)} %get-tuple-element.18) | copy-start | bytes 1437700
  97.7 4.2 %copy-start.1 = (f32[18,576]{1,0:T(8,128)S(1)}, f32[18,576]{1,0:T(8,128)}, u32[]{:S(2)}) copy-start(f32[18,576]{1,0:T(8,128)} %get-tuple-element.11) | copy-start | bytes 124420

commit v6 on v4

--- a/solution.py
+++ b/solution.py
@@ -388,70 +388,17 @@
     embed_images(x2, 3)
     each(3, lambda i: unit(other(y, i + i // 2, NY), 3 * PAIRS, PAIRS))
 
-    twin_arrived(y2)
-    unit(y2, 2 * PAIRS, 2 * PAIRS)
-
-    def cast(at, place, add=None, first=0, count=PAIRS):
-        v = s.gi[pl.ds(place * PAIRS + first, count), :]
-        if add is not None:
-            v = v + add[...].astype(F32)
-        s.xsend[at, pl.ds(first, count), :] = v.astype(BF)
-
-    for half in (0, 1):
-        first, count = IMAGE_PARTS[half]
-        cast(0, 3, first=first, count=count)
-        to, at = ((xup, s.xa), (xdown, s.xb))[half]
-        send(copy(s.xsend.at[0, pl.ds(first, count)], at, ("xa", "xb")[half], 0, to))
-
-    def image_back(at, place, half, to, add=None):
-        first, count = IMAGE_PARTS[half]
-        cast(at, place, add=add, first=first, count=count)
-        r = pl.ds(first, count)
-        send(copy(s.xsend.at[at, r], s.xr.at[at - 1, r], "xr", (at - 1) * 2 + half, to))
-
-    image_back(2, 2, 0, xdown)
-    unit(y2, 0, 2 * PAIRS)
-    image_back(1, 1, 1, xup)
-
     def text_grad(yy):
         s.gtall[...] = dot(s.w[yy], s.img[...], TN)
 
-        def out(i):
-            s.gtcsend[yy, rows(i), :] = s.gtall[rows(i, oc * TC), :].astype(BF)
-            s.gt[yy, rows(i), :] = s.gtall[rows(i, core * TC), :]
-
-        each(TC // 16, out)
+        s.gtcsend[yy] = s.gtall[at16(oc * TC, TC), :].astype(BF)
+        s.gt[yy] = s.gtall[at16(core * TC, TC), :]
 
     def send_back_twin(yy):
         send(copy(s.gtcsend.at[yy], s.gtcrecv.at[yy], "gtc", yy, twin))
 
     def back_twin_arrived(yy):
         arrived(s.gtcrecv.at[yy], "gtc", yy)
-
-    def columns_of(cc):
-        return s.w[y2, :, pl.ds(cc * TC, TC)]
-
-    @pl.when(core == 0)
-    def _():
-        s.gtcsend[y2] = dot(columns_of(1), s.img[...], TN).astype(BF)
-
-    @pl.when(core == 1)
-    def _():
-        s.gtcsend[y2] = dot(columns_of(0), s.img[...], TN).astype(BF)
-
-    send_back_twin(y2)
-
-    @pl.when(core == 0)
-    def _():
-        s.gt[y2] = dot(columns_of(0), s.img[...], TN)
-
-    @pl.when(core == 1)
-    def _():
-        s.gt[y2] = dot(columns_of(1), s.img[...], TN)
-
-    text_grad(y1)
-    send_back_twin(y1)
-    back_twin_arrived(y2)
 
     def text_back(at, yy, zz, half, dst, group, index, to, add=None):
         first, count = TEXT_PARTS[half]
@@ -466,23 +413,74 @@
     def text_back_to(at, yy, zz, half, to, add=None):
         text_back(at, yy, zz, half, lambda r: s.yr.at[at - 1, r], "yr", (at - 1) * 4 + zz * 2 + half, to, add)
 
-    for zz in (oz, zh):
-        text_back(0, y2, zz, 0, lambda r, zz=zz: s.ya.at[zz], "ya", zz, yup)
-        text_back(0, y2, zz, 1, lambda r, zz=zz: s.yb.at[zz], "yb", zz, ydown)
+    text_grad(y1)
+    send_back_twin(y1)
     text_grad(y3)
     send_back_twin(y3)
+
+    twin_arrived(y2)
+    unit(y2, 2 * PAIRS, 2 * PAIRS)
+
+    def cast(at, place, add=None, first=0, count=PAIRS):
+        v = s.gi[pl.ds(place * PAIRS + first, count), :]
+        if add is not None:
+            v = v + add[...].astype(F32)
+        s.xsend[at, pl.ds(first, count), :] = v.astype(BF)
+
+    for half in (0, 1):
+        first, count = IMAGE_PARTS[half]
+        cast(0, 3, first=first, count=count)
+        to, at = ((xup, s.xa), (xdown, s.xb))[half]
+        send(copy(s.xsend.at[0, pl.ds(first, count)], at, ("xa", "xb")[half], 0, to))
+
+    def image_back(at, place, half, to, add=None):
+        first, count = IMAGE_PARTS[half]
+        cast(at, place, add=add, first=first, count=count)
+        r = pl.ds(first, count)
+        send(copy(s.xsend.at[at, r], s.xr.at[at - 1, r], "xr", (at - 1) * 2 + half, to))
+
+    image_back(2, 2, 0, xdown)
     back_twin_arrived(y1)
     for zz in (oz, zh):
         text_back_to(1, y1, zz, 1, yup)
     back_twin_arrived(y3)
     for zz in (oz, zh):
         text_back_to(2, y3, zz, 0, ydown)
+    unit(y2, 0, 2 * PAIRS)
+    image_back(1, 1, 1, xup)
+
+    def columns_of(cc):
+        return s.w[y2, :, pl.ds(cc * TC, TC)]
+
+    @pl.when(core == 0)
+    def _():
+        s.gtcsend[y2] = dot(columns_of(1), s.img[...], TN).astype(BF)
+
+    @pl.when(core == 1)
+    def _():
+        s.gtcsend[y2] = dot(columns_of(0), s.img[...], TN).astype(BF)
+
+    send_back_twin(y2)
+
+    @pl.when(core == 0)
+    def _():
+        s.gt[y2] = dot(columns_of(0), s.img[...], TN)
+
+    @pl.when(core == 1)
+    def _():
+        s.gt[y2] = dot(columns_of(1), s.img[...], TN)
+
+    back_twin_arrived(y2)
+
+    for zz in (oz, zh):
+        text_back(0, y2, zz, 0, lambda r, zz=zz: s.ya.at[zz], "ya", zz, yup)
+        text_back(0, y2, zz, 1, lambda r, zz=zz: s.yb.at[zz], "yb", zz, ydown)
+    text_grad(y)
+    send_back_twin(y)
     arrived(s.xa, "xa")
     image_back(1, 1, 0, xup, add=s.xa)
     arrived(s.xb, "xb")
     image_back(2, 2, 1, xdown, add=s.xb)
-    text_grad(y)
-    send_back_twin(y)
     for zz in (oz, zh):
         arrived(s.ya.at[zz], "ya", zz)
         text_back_to(1, y1, zz, 0, yup, add=s.ya)

time: 103 us -> 105 us (1.019)
  Pallas kernels: 96.9 us -> 99.3 us
    pallas_call x1, Pallas kernels: 96.9 us -> 99.3 us  [per_device(): pl.pallas_call(kernel, out_shape=(jax.ShapeDtypeStruct((PAIRS, HALF), F32...]
where the time goes in v6:
time: 105 us
  Pallas kernels  99.3 us (95%)
  local copies, waits for them, and re-layouts  4.81 us (5%)
    pallas_call x1, Pallas kernels, per_device(): pl.pallas_call(kernel, out_shape=(jax.ShapeDtypeStruct((PAIRS, HALF), F32...  99.3 us
    unnamed x8, local copies, waits for them, and re-layouts  4.81 us

profile of v6, /device:TPU:1, one launch (start us, length us, event | category | flops | bytes accessed | tf_op | source)
XLA Modules:
  0.0 104.8 jit_solution(9578432610589144945)
XLA Ops:
  0.6 99.3 %shard_map.75 = (f32[208,576]{1,0:T(8,128)}, f32[18,576]{1,0:T(8,128)}, f32[208,576]{1,0:T(8,128)}, f32[18,576]{1,0:T(8,128)}) custom-call(bf16[208,1152]{1,0:T(8,128)(2,1)} %img_feat.1, bf16[576,1152]{1,0:T(8,128)(2,1)} %bitcast.3, bf16[208,1152]{1,0:T(8,128)(2,1)} %txt_feat.1, bf16[576,1152]{1,0:T(8,128)(2,1)} %txt_head.1), custom_call_target="tpu_custom_call" | custom-call | flops 14000000000 | bytes 5000000 | tf_op jit(solution)/shard_map/pallas_call | solution.py:710
  100.0 0.0 copy-start
  100.0 0.0 copy-start.1
  100.0 1.9 %copy.12 = f32[208,576]{1,0:T(8,128)} copy(f32[208,576]{1,0:T(8,128)} %get-tuple-element.16) | data formatting | bytes 958464
  101.9 1.5 %copy.13 = f32[18,576]{1,0:T(8,128)} copy(f32[18,576]{1,0:T(8,128)} %get-tuple-element.17) | data formatting | bytes 82944
  103.4 0.0 copy-done
  103.4 0.8 copy.14
  104.2 0.0 copy-done.1
  104.2 0.6 copy.15
Async XLA Ops:
  100.0 3.4 %copy-start = (f32[208,576]{1,0:T(8,128)S(1)}, f32[208,576]{1,0:T(8,128)}, u32[]{:S(2)}) copy-start(f32[208,576]{1,0:T(8,128)} %get-tuple-element.18) | copy-start | bytes 1437700
  100.0 4.2 %copy-start.1 = (f32[18,576]{1,0:T(8,128)S(1)}, f32[18,576]{1,0:T(8,128)}, u32[]{:S(2)}) copy-start(f32[18,576]{1,0:T(8,128)} %get-tuple-element.11) | copy-start | bytes 124420

commit v7 on v4

--- a/solution.py
+++ b/solution.py
@@ -333,6 +333,12 @@
     each(IMGS // 16, zero)
     forward_image(m)
 
+    for half in (0, 1):
+        text_arrived(y, oz, half)
+        send_text(y, oz, yup, half)
+        send_text(y, oz, ydown, half)
+    send_twin(y, oz)
+
     image_arrived(x, om)
     send_image(x, om, xup)
     send_image(x, om, xdown)
@@ -346,11 +352,6 @@
 
     embed_images(x, 0, own=True)
 
-    for half in (0, 1):
-        text_arrived(y, oz, half)
-        send_text(y, oz, yup, half)
-        send_text(y, oz, ydown, half)
-    send_twin(y, oz)
     forward_text(zh)
 
     def unit(yy, first, count, own=False):

time: 103 us -> 101 us (0.981)
  Pallas kernels: 96.9 us -> 94.9 us
    pallas_call x1, Pallas kernels: 96.9 us -> 94.9 us  [per_device(): pl.pallas_call(kernel, out_shape=(jax.ShapeDtypeStruct((PAIRS, HALF), F32...]
where the time goes in v7:
time: 101 us; the launch traced here: 100 us
  Pallas kernels  94.9 us (94%)
  local copies, waits for them, and re-layouts  4.81 us (5%)
    pallas_call x1, Pallas kernels, per_device(): pl.pallas_call(kernel, out_shape=(jax.ShapeDtypeStruct((PAIRS, HALF), F32...  94.9 us
    unnamed x8, local copies, waits for them, and re-layouts  4.81 us

profile of v7, /device:TPU:1, one launch (start us, length us, event | category | flops | bytes accessed | tf_op | source)
XLA Modules:
  0.0 100.4 jit_solution(9497676999201514646)
XLA Ops:
  0.6 94.9 %shard_map.75 = (f32[208,576]{1,0:T(8,128)}, f32[18,576]{1,0:T(8,128)}, f32[208,576]{1,0:T(8,128)}, f32[18,576]{1,0:T(8,128)}) custom-call(bf16[208,1152]{1,0:T(8,128)(2,1)} %img_feat.1, bf16[576,1152]{1,0:T(8,128)(2,1)} %bitcast.3, bf16[208,1152]{1,0:T(8,128)(2,1)} %txt_feat.1, bf16[576,1152]{1,0:T(8,128)(2,1)} %txt_head.1), custom_call_target="tpu_custom_call" | custom-call | flops 14000000000 | bytes 5000000 | tf_op jit(solution)/shard_map/pallas_call | solution.py:713
  95.6 0.0 copy-start
  95.6 0.0 copy-start.1
  95.6 1.9 %copy.12 = f32[208,576]{1,0:T(8,128)} copy(f32[208,576]{1,0:T(8,128)} %get-tuple-element.16) | data formatting | bytes 958464
  97.5 1.5 %copy.13 = f32[18,576]{1,0:T(8,128)} copy(f32[18,576]{1,0:T(8,128)} %get-tuple-element.17) | data formatting | bytes 82944
  99.0 0.0 copy-done
  99.0 0.8 copy.14
  99.8 0.0 copy-done.1
  99.8 0.6 copy.15
Async XLA Ops:
  95.6 3.4 %copy-start = (f32[208,576]{1,0:T(8,128)S(1)}, f32[208,576]{1,0:T(8,128)}, u32[]{:S(2)}) copy-start(f32[208,576]{1,0:T(8,128)} %get-tuple-element.18) | copy-start | bytes 1437700
  95.6 4.2 %copy-start.1 = (f32[18,576]{1,0:T(8,128)S(1)}, f32[18,576]{1,0:T(8,128)}, u32[]{:S(2)}) copy-start(f32[18,576]{1,0:T(8,128)} %get-tuple-element.11) | copy-start | bytes 124420
